TPU v7x, 256 devices: a whole 4x4x8 slice. The times are simulated.
256 devices in a mesh: vol: 16 (over y_hi, x, core), surf: 16 (over z, y_lo).
Axes of the slice: x: 4, y: 4 (y_hi: 2, y_lo: 2; y = y_hi * 2 + y_lo), z: 8, core: 2. Of those that a mesh axis runs over, the one named last changes fastest.
Arguments:
- surface_points: float32 [3, 131072], P(None, ('vol', 'surf')), may hold values from -3 to 11
- surface_shift: float32 [3, 131072], P(None, ('vol', 'surf')), may hold values from -1.25 to 1.25
- facet_nodes: int32 [512, 3, 512], P(('vol', 'surf')), may hold values from 0 to 255, as said below
- volume_points: float32 [3, 131072], P(None, 'vol'), may hold values from -5 to 13
- near_wall: int32 [131072], P('vol'), may hold values from 0 to 1
- candidates: int32 [1024, 16], P('vol'), may hold values from -1 to 511, as said below
Outputs:
- displacement: float32 [3, 131072], P(None, ('vol', 'surf'))
- wall_distance: float32 [131072], P(('vol', 'surf'))
Inputs may be any that keep to these rules, and one draw needn't show every extreme that they name: Corner k of facet f of leaf l is surface node l * 256 + facet_nodes[l, k, f]; the three corners of a facet are distinct nodes of that leaf. `candidates`: in each row the real leaf ids come first, are distinct, and -1 fills the rest; every row holds at least one real id.
All inputs are finite; a program needn't handle non-finite values.
Results may differ from a plain program's by a relative error of at most 0.0003.
Values sent between devices are 32-bit elements; how exact they have to be, the bound alone decides.
A program may use at most 64 MiB of HBM per device.

v0:
```python
import jax
import jax.numpy as jnp
from jax import lax
from jax.sharding import PartitionSpec as P

smoothing = 0.01
big_value = 1e30
weigh_group = 8
facet_group = 4


def minus3(first_vec, second_vec):
    return [
        first_vec[0] - second_vec[0],
        first_vec[1] - second_vec[1],
        first_vec[2] - second_vec[2],
    ]


def dot3(first_vec, second_vec):
    return (
        first_vec[0] * second_vec[0] + first_vec[1] * second_vec[1] + first_vec[2] * second_vec[2]
    )


def cross3(first_vec, second_vec):
    return [
        first_vec[1] * second_vec[2] - first_vec[2] * second_vec[1],
        first_vec[2] * second_vec[0] - first_vec[0] * second_vec[2],
        first_vec[0] * second_vec[1] - first_vec[1] * second_vec[0],
    ]


def segment_squares(offset_vec, edge_vec, inverse_length):
    fraction = jnp.clip(dot3(offset_vec, edge_vec) * inverse_length, 0.0, 1.0)
    remain = [
        offset_vec[0] - fraction * edge_vec[0],
        offset_vec[1] - fraction * edge_vec[1],
        offset_vec[2] - fraction * edge_vec[2],
    ]
    return dot3(remain, remain)


def facet_squares(points, corners):
    probe_point = [points[..., 0, :, None], points[..., 1, :, None], points[..., 2, :, None]]
    vert_a = [corners[..., 0, None, :], corners[..., 1, None, :], corners[..., 2, None, :]]
    vert_b = [corners[..., 3, None, :], corners[..., 4, None, :], corners[..., 5, None, :]]
    vert_c = [corners[..., 6, None, :], corners[..., 7, None, :], corners[..., 8, None, :]]
    edge_ab = minus3(vert_b, vert_a)
    edge_bc = minus3(vert_c, vert_b)
    edge_ca = minus3(vert_a, vert_c)
    normal = cross3(edge_ab, minus3(vert_c, vert_a))
    inverse_normal = 1.0 / dot3(normal, normal)
    side_ab = cross3(normal, edge_ab)
    side_bc = cross3(normal, edge_bc)
    side_ca = cross3(normal, edge_ca)
    from_a = minus3(probe_point, vert_a)
    from_b = minus3(probe_point, vert_b)
    from_c = minus3(probe_point, vert_c)
    inside = (
        (dot3(from_a, side_ab) >= 0.0)
        & (dot3(from_b, side_bc) >= 0.0)
        & (dot3(from_c, side_ca) >= 0.0)
    )
    height = dot3(from_a, normal)
    plane_sq = height * height * inverse_normal
    edge_sq = jnp.minimum(
        segment_squares(from_a, edge_ab, 1.0 / dot3(edge_ab, edge_ab)),
        segment_squares(from_b, edge_bc, 1.0 / dot3(edge_bc, edge_bc)),
    )
    edge_sq = jnp.minimum(edge_sq, segment_squares(from_c, edge_ca, 1.0 / dot3(edge_ca, edge_ca)))
    return jnp.where(inside, plane_sq, edge_sq)


def inverse_square(points, others):
    distance_sq = (others[..., 0, :, None] - points[..., 0, None, :]) ** 2
    distance_sq = distance_sq + (others[..., 1, :, None] - points[..., 1, None, :]) ** 2
    distance_sq = distance_sq + (others[..., 2, :, None] - points[..., 2, None, :]) ** 2
    inverse = 1.0 / (distance_sq + smoothing)
    return inverse * inverse


def weigh_sums(weight, shift):
    return jnp.stack(
        [
            jnp.sum(weight * shift[..., 0, :, None], axis=-2),
            jnp.sum(weight * shift[..., 1, :, None], axis=-2),
            jnp.sum(weight * shift[..., 2, :, None], axis=-2),
            jnp.sum(weight, axis=-2),
        ],
        axis=-2,
    )


def corner_table(moved_nodes, facet_nodes):
    leaves = facet_nodes.shape[0]
    per_leaf = jnp.moveaxis(moved_nodes.reshape(3, leaves, -1), 1, 0)
    pieces = []
    for corner in range(3):
        gather_index = jnp.broadcast_to(
            facet_nodes[:, corner : corner + 1, :], (leaves, 3, facet_nodes.shape[2])
        )
        pieces.append(jnp.take_along_axis(per_leaf, gather_index, axis=2))
    return jnp.concatenate(pieces, axis=1)


def pair_list(usable, leaf_rows, group_size):
    slot_count = usable.shape[1]
    flat_usable = usable.reshape(-1)
    pair_count = jnp.sum(flat_usable.astype(jnp.int32))
    pair_order = jnp.argsort(jnp.where(flat_usable, 0, 1), stable=True)
    filler = jnp.zeros((group_size,), jnp.int32)
    pair_blocks = jnp.concatenate([pair_order // slot_count, filler])
    pair_leaves = jnp.concatenate([leaf_rows.reshape(-1)[pair_order], filler])
    return (pair_blocks, pair_leaves, pair_count)


def to_blocks(points, block_count):
    block_len = points.shape[1] // block_count
    return jnp.moveaxis(points.reshape(3, block_count, block_len), 1, 0)


def near_sums(points, usable, leaf_rows, node_table):
    block_count = usable.shape[0]
    block_points = to_blocks(points, block_count)
    pair_blocks, pair_leaves, pair_count = pair_list(usable, leaf_rows, weigh_group)
    rounds = (pair_count + weigh_group - 1) // weigh_group
    initial = jnp.zeros((block_count, 4, block_points.shape[2]), jnp.float32)

    def near_one_round(round_index, result):
        offset = round_index * weigh_group
        chosen_blocks = lax.dynamic_slice_in_dim(pair_blocks, offset, weigh_group)
        chosen_leaves = lax.dynamic_slice_in_dim(pair_leaves, offset, weigh_group)
        in_use = offset + jnp.arange(weigh_group) < pair_count
        chosen_nodes = node_table[chosen_leaves]
        weight = inverse_square(block_points[chosen_blocks], chosen_nodes[:, :3])
        terms_here = weigh_sums(weight, chosen_nodes[:, 3:])
        terms_here = jnp.where(in_use[:, None, None], terms_here, 0.0)
        return result.at[chosen_blocks].add(terms_here)

    result = lax.fori_loop(0, rounds, near_one_round, initial)
    return jnp.moveaxis(result, 0, 1).reshape(4, -1)


def far_sums(points, cands, leaf_global, centers, center_shift, leaf_len):
    block_points = to_blocks(points, cands.shape[0])
    listed = jnp.any(cands[:, :, None] == leaf_global[None, None, :], axis=1)
    weight = inverse_square(block_points, centers) * leaf_len
    weight = jnp.where(listed[:, :, None], 0.0, weight)
    terms_here = weigh_sums(weight, center_shift)
    return jnp.moveaxis(terms_here, 0, 1).reshape(4, -1)


def nearest_squares(points, usable, leaf_rows, leaf_table):
    block_count = usable.shape[0]
    block_points = to_blocks(points, block_count)
    block_len = block_points.shape[2]
    pair_blocks, pair_leaves, pair_count = pair_list(usable, leaf_rows, facet_group)
    rounds = (pair_count + facet_group - 1) // facet_group
    initial = jnp.full((block_count, block_len), big_value, jnp.float32)

    def nearest_one_round(round_index, result):
        offset = round_index * facet_group
        chosen_blocks = lax.dynamic_slice_in_dim(pair_blocks, offset, facet_group)
        chosen_leaves = lax.dynamic_slice_in_dim(pair_leaves, offset, facet_group)
        in_use = offset + jnp.arange(facet_group) < pair_count
        squared = facet_squares(block_points[chosen_blocks], leaf_table[chosen_leaves])
        closest = jnp.where(in_use[:, None], jnp.min(squared, axis=2), big_value)
        return result.at[chosen_blocks].min(closest)

    result = lax.fori_loop(0, rounds, nearest_one_round, initial)
    return result.reshape(-1)


def leaf_moments(node_table):
    centers = jnp.transpose(jnp.mean(node_table[:, :3], axis=2))
    center_shift = jnp.transpose(jnp.mean(node_table[:, 3:], axis=2))
    return (centers, center_shift)


def body(surface_points, surface_shift, facet_nodes, volume_points, near_wall, candidates):
    surf_count = lax.axis_size("surf")
    surf_rank = lax.axis_index("surf")
    leaf_dev = facet_nodes.shape[0]
    leaf_len = surface_points.shape[1] // leaf_dev
    total_vol = volume_points.shape[1]
    share_len = total_vol // surf_count
    block_len = total_vol // candidates.shape[0]
    share_blocks = share_len // block_len
    own_nodes = jnp.concatenate(
        [
            jnp.moveaxis(surface_points.reshape(3, leaf_dev, leaf_len), 1, 0),
            jnp.moveaxis(surface_shift.reshape(3, leaf_dev, leaf_len), 1, 0),
        ],
        axis=1,
    )
    moved_surface = surface_points + surface_shift
    corners = corner_table(moved_surface, facet_nodes)
    node_start = surf_rank * share_len
    own_flags = lax.dynamic_slice_in_dim(near_wall, node_start, share_len)
    node_table = lax.all_gather(own_nodes, ("vol", "surf"), axis=0, tiled=True)
    leaf_table = lax.all_gather(corners, ("vol", "surf"), axis=0, tiled=True)
    centers, center_shift = leaf_moments(node_table)
    own_points = lax.dynamic_slice_in_dim(volume_points, node_start, share_len, 1)
    own_cands = lax.dynamic_slice_in_dim(candidates, surf_rank * share_blocks, share_blocks, 0)
    leaf_global = jnp.arange(node_table.shape[0], dtype=jnp.int32)
    safe_rows = jnp.maximum(own_cands, 0)
    weighted = near_sums(own_points, own_cands >= 0, safe_rows, node_table)
    weighted = weighted + far_sums(
        own_points, own_cands, leaf_global, centers, center_shift, leaf_len
    )
    displacement = weighted[:3] / weighted[3:4]
    moved_nodes = own_points + displacement
    block_near = jnp.max(own_flags.reshape(share_blocks, block_len), axis=1) > 0
    usable = (own_cands >= 0) & block_near[:, None]
    squares = nearest_squares(moved_nodes, usable, safe_rows, leaf_table)
    wall_distance = jnp.where(own_flags == 1, jnp.sqrt(squares), 0.0)
    return (displacement, wall_distance)


def solution(mesh):
    placed = (
        P(None, ("vol", "surf")),
        P(None, ("vol", "surf")),
        P(("vol", "surf"), None, None),
        P(None, "vol"),
        P("vol"),
        P("vol", None),
    )
    return jax.shard_map(
        body,
        mesh=mesh,
        in_specs=placed,
        out_specs=(P(None, ("vol", "surf")), P(("vol", "surf"))),
        check_vma=False,
    )
```

profile of v0, /device:TPU:99, one launch (start us, length us, event | category | flops | bytes accessed | tf_op | source)
XLA Modules:
  0.0 1623.0 jit_solution(6605452299637330925)
XLA Ops:
  7.2 1.3 pad_maximum_fusion.1
  11.6 30.1 %gather_fusion.8 = f32[3072]{0:T(1024)S(1)} fusion(f32[2,3,256]{2,0,1:T(2,128)S(1)} %bitcast.305, s32[3072]{0:T(1024)S(1)} %reshape.206), kind=kCustom, calls=%fused_computation.6.clone | custom fusion | bytes 61440 | tf_op jit(solution)/shard_map/jit(take_along_axis)/gather | solution.py:103
  41.7 30.1 %gather_fusion.7 = f32[3072]{0:T(1024)S(1)} fusion(f32[2,3,256]{2,0,1:T(2,128)S(1)} %bitcast.306, s32[3072]{0:T(1024)S(1)} %reshape.201), kind=kCustom, calls=%fused_computation.5.clone | custom fusion | bytes 61440 | tf_op jit(solution)/shard_map/jit(take_along_axis)/gather | solution.py:103
  71.8 30.1 %gather_fusion.6 = f32[3072]{0:T(1024)S(1)} fusion(f32[2,3,256]{2,0,1:T(2,128)S(1)} %bitcast.307, s32[3072]{0:T(1024)S(1)} %reshape.196), kind=kCustom, calls=%fused_computation.2.clone | custom fusion | bytes 61440 | tf_op jit(solution)/shard_map/jit(take_along_axis)/gather | solution.py:103
  105.9 2.1 sort.32
  108.0 2.0 sort.31
  112.7 613.2 %all-gather.3.cloned.1.call-done = f32[512,6,256]{2,1,0:T(8,128)} async-done(((f32[2,6,256]{2,1,0:T(8,128)}), f32[512,6,256]{2,1,0:T(8,128)}) %all-gather.3.cloned.1.call-update) | async-done | bytes 3145744 | tf_op jit(solution)/shard_map/all_gather | solution.py:201
  725.9 4.7 slice_reduce_fusion
  732.5 42.6 %while.20 = (s32[]{:T(128)}, f32[4,4,128]{2,1,0:T(4,128)S(1)}, s32[]{:T(128)}, s32[72]{0:T(128)S(1)}, s32[]{:T(128)}, /*index=5*/s32[72]{0:T(128)S(1)}, f32[512,...) while((s32[]{:T(128)}, f32[4,4,128]{2,1,0:T(4,128)S(1)}, ...), condition=%wide.region_8.9_spmd, body=%wide.region_2.8_spmd.sunk | while | flops 4737094 | bytes 545255 | solution.py:141
  732.6 2.7 gather_fusion
  736.1 2.0 multiply_reduce_fusion.7
  739.7 2.8 gather_fusion
  743.2 2.0 multiply_reduce_fusion.7
  746.8 2.7 gather_fusion
  750.3 2.0 multiply_reduce_fusion.7
  753.9 2.7 gather_fusion
  757.4 2.0 multiply_reduce_fusion.7
  761.0 2.7 gather_fusion
  764.5 2.0 multiply_reduce_fusion.7
  768.1 2.7 gather_fusion
  771.6 2.0 multiply_reduce_fusion.7
  776.5 682.2 %all-gather.5.cloned.1.call-done = f32[512,9,512]{2,1,0:T(8,128)} async-done(((f32[2,9,512]{2,1,0:T(8,128)}), f32[512,9,512]{2,1,0:T(8,128)}) %all-gather.5.cloned.1.call-update) | async-done | bytes 9437200 | tf_op jit(solution)/shard_map/all_gather | solution.py:202
  1458.7 156.1 %while.21 = (s32[]{:T(128)}, f32[4,128]{1,0:T(4,128)S(1)}, s32[]{:T(128)}, s32[68]{0:T(128)S(1)}, s32[]{:T(128)}, /*index=5*/f32[4,3,128]{2,1,0:T(4,128)S(1)}, s...) while((s32[]{:T(128)}, f32[4,128]{1,0:T(4,128)S(1)}, ...), condition=%wide.region_22.24_spmd, body=%wide.region_19.23_spmd.sunk | while | flops 24795684 | bytes 1618759 | solution.py:171
  1458.8 6.3 gather_fusion.2
  1466.4 4.1 fusion.82
  1471.8 6.3 gather_fusion.2
  1479.4 4.1 fusion.82
  1484.8 6.3 gather_fusion.2
  1492.4 4.1 fusion.82
  1497.8 6.3 gather_fusion.2
  1505.4 4.1 fusion.82
  1510.8 6.3 gather_fusion.2
  1518.5 4.1 fusion.82
  1523.9 6.3 gather_fusion.2
  1531.5 4.1 fusion.82
  1536.9 6.3 gather_fusion.2
  1544.5 4.1 fusion.82
  1549.9 6.3 gather_fusion.2
  1557.5 4.1 fusion.82
  1562.9 6.3 gather_fusion.2
  1570.5 4.1 fusion.82
  1575.9 6.3 gather_fusion.2
  1583.5 4.1 fusion.82
  1588.9 6.3 gather_fusion.2
  1596.5 4.1 fusion.82
  1601.9 6.3 gather_fusion.2
  1609.5 4.1 fusion.82
  1614.8 1.3 bitcast_select_fusion
  (695 shorter events, 52.7 us)
Async XLA Ops:
  7.2 718.8 %all-gather.3.cloned.1.call-start = ((), (), s32[]{:S(2)}) async-start(), calls=%async_computation | async-start | bytes 4210688 | tf_op jit(solution)/shard_map/all_gather | solution.py:201
  8.6 1450.2 %all-gather.5.cloned.1.call-start = ((), (), s32[]{:S(2)}) async-start(), calls=%async_computation.1 | async-start | bytes 16842752 | tf_op jit(solution)/shard_map/all_gather | solution.py:202
  71.8 31.7 %copy-start = (s32[64,16]{0,1:T(8,128)S(1)}, s32[64,16]{0,1:T(8,128)}, u32[]{:S(2)}) copy-start(s32[64,16]{0,1:T(8,128)} %param.17) | copy-start | bytes 12292
Sparse Core Ops, SparseCore 0:
  9.9 715.9 all-gather.2
  727.8 730.8 all-gather.4
where the time goes:
time: 1620 us
  waiting for transfers between devices  1300 us (80%)
  local copies, waits for them, and re-layouts  199 us (12%)
  other arithmetic  108 us (7%)
    all_gather x1, waiting for transfers between devices, body(): leaf_table = lax.all_gather(corners, ('vol', 'surf'), axis=0, tiled=True)  682 us
    all_gather x1, waiting for transfers between devices, body(): node_table = lax.all_gather(own_nodes, ('vol', 'surf'), axis=0, tiled=True)  613 us
    gather x9, local copies, waits for them, and re-layouts, corner_table(): pieces.append(jnp.take_along_axis(per_leaf, gather_index, axis=2))  90.2 us
    gather x12, local copies, waits for them, and re-layouts, nearest_one_round(): leaf_table[chosen_leaves]  75.9 us
    reduce_min x12, other arithmetic, nearest_one_round(): closest = jnp.where(in_use[:, None], jnp.min(squared, axis=2), big_value)  48.8 us
  transfers between devices with their start and end apart: 2, of which 2 were waited for; matrix products, arithmetic and copies ran while one was open for 9% of the time, Pallas kernels for 0%

commit v1 on v0

v1 whole, which is shorter than its diff:
```python
import functools

import jax
import jax.numpy as jnp
from jax import lax
from jax.experimental import pallas as pl
from jax.experimental.pallas import tpu as pltpu
from jax.sharding import PartitionSpec as P

MESH = pl.DeviceIdType.MESH
smoothing = 0.01
big_value = 1e30

NX, NY, NZ = 4, 4, 8
SIZES = {"x": NX, "y": NY, "z": NZ}
ORDERS = (("z", "y", "x"), ("x", "z", "y"), ("y", "x", "z"))
LEAF = 256
CHIPS = NX * NY * NZ
LEAVES = 4 * CHIPS
LANES = 128


def coords_of(vol, surf):
    return {
        "x": (vol // 2) % NX,
        "y": (vol // (2 * NX)) * 2 + surf % 2,
        "z": surf // 2,
        "c": vol % 2,
    }


def mesh_id(c):
    return ((c["y"] // 2) * NX + c["x"]) * 2 + c["c"], c["z"] * 2 + c["y"] % 2


def shifted(c, axis, k):
    n = SIZES[axis]
    return {**c, axis: lax.rem(c[axis] + (k % n), n)}


def place(c, order):
    a, b, d = order
    return ((c["c"] * SIZES[d] + c[d]) * SIZES[b] + c[b]) * SIZES[a] + c[a]


def chunk_of(c, order, phase):
    a, b, _ = order
    length = (1, SIZES[a], SIZES[a] * SIZES[b])[phase]
    start = place(c, order)
    return (start // length) * length, length


def gather_kernel(points_ref, shift_ref, facets_ref, table, moments, mom_own, mom_z, mom_y, mom_c,
                  send_sem, recv_sem, core_send, core_recv, mom_send, mom_recv):
    me = coords_of(lax.axis_index("vol"), lax.axis_index("surf"))
    sibling = {**me, "c": 1 - me["c"]}
    partners = [sibling]
    for axis, n in SIZES.items():
        partners += [shifted(me, axis, k) for k in range(1, n)]
    barrier = pltpu.get_barrier_semaphore()
    for other in partners:
        pl.semaphore_signal(barrier, inc=1, device_id=mesh_id(other), device_id_type=MESH)

    own = [place(me, order) * 2 for order in ORDERS]
    for leaf in range(2):
        for half in range(2):
            lanes = pl.ds(leaf * LEAF + half * LANES, LANES)
            for c in range(3):
                table[0, own[0] + leaf, pl.ds(2 * c + half, 1), :] = points_ref[pl.ds(c, 1), lanes]
            table[0, own[0] + leaf, pl.ds(6 + half, 1), :] = shift_ref[pl.ds(0, 1), lanes]
            table[1, own[1] + leaf, pl.ds(0 + half, 1), :] = shift_ref[pl.ds(1, 1), lanes]
            table[1, own[1] + leaf, pl.ds(2 + half, 1), :] = shift_ref[pl.ds(2, 1), lanes]
        for quarter in range(4):
            lanes = pl.ds(quarter * LANES, LANES)
            for k, (part, row) in enumerate(((1, 4), (2, 0), (2, 4))):
                table[part, own[part] + leaf, pl.ds(row + quarter, 1), :] = (
                    facets_ref[leaf, pl.ds(k, 1), lanes].astype(jnp.float32)
                )
    lane = lax.broadcasted_iota(jnp.int32, (3, LANES), 1)
    my_lane = ((me["c"] * NY + me["y"]) * NZ + me["z"]) * 2
    for row, ref in ((0, points_ref), (3, shift_ref)):
        tile = jnp.zeros((3, LANES), jnp.float32)
        for leaf in range(2):
            mean = jnp.sum(ref[:, pl.ds(leaf * LEAF, LEAF)], axis=1, keepdims=True) * (1.0 / LEAF)
            tile = jnp.where(lane == my_lane + leaf, mean, tile)
        mom_own[pl.ds(row, 3), :] = tile
    mom_own[pl.ds(6, 2), :] = jnp.zeros((2, LANES), jnp.float32)
    pl.semaphore_wait(barrier, len(partners))

    sent = []

    def push(part, start, length, to, s_sem, r_sem):
        where = table.at[part, pl.ds(start * 2, length * 2)]
        copy = pltpu.make_async_remote_copy(
            src_ref=where, dst_ref=where, send_sem=s_sem, recv_sem=r_sem,
            device_id=mesh_id(to), device_id_type=MESH,
        )
        copy.start()
        sent.append(copy)

    def arrived(part, start, length, frm, s_sem, r_sem):
        where = table.at[part, pl.ds(start * 2, length * 2)]
        pltpu.make_async_remote_copy(
            src_ref=where, dst_ref=where, send_sem=s_sem, recv_sem=r_sem,
            device_id=mesh_id(frm), device_id_type=MESH,
        ).wait_recv()

    steps = []
    for order in ORDERS:
        steps.append([(ph, s) for ph in range(3) for s in range(1, SIZES[order[ph]] // 2 + 1)])
    core_slot = [0, 0, 0]
    core_in = []

    def to_sibling(part, c, phase, first=0, count=None):
        start, length = chunk_of(c, ORDERS[part], phase)
        theirs, _ = chunk_of({**c, "c": 1 - me["c"]}, ORDERS[part], phase)
        count = length if count is None else count
        slot = core_slot[part]
        core_slot[part] += 1
        push(part, start + first, count, sibling, core_send.at[part, slot], core_recv.at[part, slot])
        core_in.append((part, theirs + first, count, slot))

    def pieces(part, phase, s):
        axis = ORDERS[part][phase]
        n = SIZES[axis]
        _, length = chunk_of(me, ORDERS[part], phase)
        if s < n // 2:
            return [(1, first_, 0, length) for first_ in (s - 1,)] + [(-1, s - 1, 0, length)]
        if length == 1:
            return [(1, s - 1, 0, 1)]
        return [(1, s - 1, 0, length // 2), (-1, s - 1, length // 2, length // 2)]

    def issue(part, index):
        phase, s = steps[part][index]
        axis = ORDERS[part][phase]
        for way, back, first, count in pieces(part, phase, s):
            origin = shifted(me, axis, -way * back)
            start, _ = chunk_of(origin, ORDERS[part], phase)
            d = 0 if way > 0 else 1
            push(part, start + first, count, shifted(me, axis, way),
                 send_sem.at[part, index, d], recv_sem.at[part, index, d])

    def collect(part, index):
        phase, s = steps[part][index]
        axis = ORDERS[part][phase]
        for way, back, first, count in pieces(part, phase, s):
            origin = shifted(me, axis, -way * (back + 1))
            start, _ = chunk_of(origin, ORDERS[part], phase)
            d = 0 if way > 0 else 1
            arrived(part, start + first, count, shifted(me, axis, -way),
                    send_sem.at[part, index, d], recv_sem.at[part, index, d])

    def hand_on(part, index):
        phase, s = steps[part][index]
        axis = ORDERS[part][phase]
        if phase == 0:
            if s == SIZES[axis] // 2:
                to_sibling(part, me, 1)
            return
        for way, back, first, count in pieces(part, phase, s):
            to_sibling(part, shifted(me, axis, -way * (back + 1)), phase, first, count)

    def mom_copies(src, dst, others, slot0):
        out = []
        for k, (other, row) in enumerate(others):
            out.append(pltpu.make_async_remote_copy(
                src_ref=src, dst_ref=dst.at[row], send_sem=mom_send.at[slot0 + k],
                recv_sem=mom_recv.at[slot0 + k], device_id=mesh_id(other), device_id_type=MESH,
            ))
        return out

    z_copies = mom_copies(mom_own, mom_z, [(shifted(me, "z", k), k - 1) for k in range(1, NZ)], 0)
    for part in range(3):
        issue(part, 0)
    for copy in z_copies:
        copy.start()
    n_steps = len(steps[0])
    later = []
    for index in range(n_steps):
        for part in range(3):
            collect(part, index)
            if index + 1 < n_steps:
                issue(part, index + 1)
            hand_on(part, index)
        if index == 0:
            total = mom_own[...]
            for k, copy in enumerate(z_copies):
                copy.wait()
                total = total + mom_z[k]
            mom_own[...] = total
            later = mom_copies(mom_own, mom_y, [(shifted(me, "y", k), k - 1) for k in range(1, NY)], 7)
            for copy in later:
                copy.start()
        elif index == 2:
            total = mom_own[...]
            for k, copy in enumerate(later):
                copy.wait()
                total = total + mom_y[k]
            mom_own[...] = total
            later = mom_copies(mom_own, mom_c, [(sibling, 0)], 10)
            later[0].start()
        elif index == 3:
            later[0].wait()
            mom_own[...] = mom_own[...] + mom_c[0]
            moments[pl.ds(me["x"], 1)] = mom_own[...][None]
            later = []
            for k in range(1, NX):
                copy = pltpu.make_async_remote_copy(
                    src_ref=mom_own, dst_ref=moments.at[me["x"]], send_sem=mom_send.at[10 + k],
                    recv_sem=mom_recv.at[10 + k], device_id=mesh_id(shifted(me, "x", k)),
                    device_id_type=MESH,
                )
                copy.start()
                later.append(copy)
        elif index == 5:
            for k in range(1, NX):
                frm = shifted(me, "x", -k)
                pltpu.make_async_remote_copy(
                    src_ref=mom_own, dst_ref=moments.at[frm["x"]], send_sem=mom_send.at[10 + k],
                    recv_sem=mom_recv.at[10 + k], device_id=mesh_id(frm), device_id_type=MESH,
                ).wait_recv()
            for copy in later:
                copy.wait_send()
    for part, start, count, slot in core_in:
        arrived(part, start, count, sibling, core_send.at[part, slot], core_recv.at[part, slot])
    for copy in sent:
        copy.wait_send()


def gather(points, shift, facets):
    f32 = jnp.float32
    vmem = pl.BlockSpec(memory_space=pltpu.VMEM)
    return pl.pallas_call(
        gather_kernel,
        out_shape=(
            jax.ShapeDtypeStruct((3, LEAVES, 8, LANES), f32),
            jax.ShapeDtypeStruct((NX, 8, LANES), f32),
        ),
        in_specs=[vmem] * 3,
        out_specs=(vmem, vmem),
        scratch_shapes=[
            pltpu.VMEM((8, LANES), f32),
            pltpu.VMEM((7, 8, LANES), f32),
            pltpu.VMEM((3, 8, LANES), f32),
            pltpu.VMEM((1, 8, LANES), f32),
            pltpu.SemaphoreType.DMA((3, 8, 2)),
            pltpu.SemaphoreType.DMA((3, 8, 2)),
            pltpu.SemaphoreType.DMA((3, 24)),
            pltpu.SemaphoreType.DMA((3, 24)),
            pltpu.SemaphoreType.DMA((14,)),
            pltpu.SemaphoreType.DMA((14,)),
        ],
        compiler_params=pltpu.CompilerParams(
            collective_id=0, has_side_effects=True, vmem_limit_bytes=40 * 2**20
        ),
    )(points, shift, facets)


def dot3(a, b):
    return a[0] * b[0] + a[1] * b[1] + a[2] * b[2]


def minus3(a, b):
    return [a[0] - b[0], a[1] - b[1], a[2] - b[2]]


def cross3(a, b):
    return [a[1] * b[2] - a[2] * b[1], a[2] * b[0] - a[0] * b[2], a[0] * b[1] - a[1] * b[0]]


def leaf_places(leaf):
    device, within = leaf // 2, leaf % 2
    c = coords_of(device // 16, device % 16)
    return [place(c, order) * 2 + within for order in ORDERS]


def leaf_ids(x):
    lane = lax.broadcasted_iota(jnp.int32, (1, LANES), 1)
    z = (lane // 2) % NZ
    y = (lane // (2 * NZ)) % NY
    core = lane // (2 * NZ * NY)
    vol = ((y // 2) * NX + x) * 2 + core
    return (vol * 16 + z * 2 + y % 2) * 2 + lane % 2


PG = 32
CONST = 20


def facet_constants(a, b, c):
    ab, ac = minus3(b, a), minus3(c, a)
    normal = cross3(ab, ac)
    ab_len = jnp.sqrt(dot3(ab, ab))
    inv_ab = 1.0 / ab_len
    inv_n = lax.rsqrt(dot3(normal, normal))
    e1 = [q * inv_ab for q in ab]
    n = [q * inv_n for q in normal]
    e2 = cross3(n, e1)
    cx, cy = dot3(ac, e1), dot3(ac, e2)
    bc_x = cx - ab_len
    bc_len = jnp.sqrt(bc_x * bc_x + cy * cy)
    ac_len = jnp.sqrt(cx * cx + cy * cy)
    inv_bc, inv_ac = 1.0 / bc_len, 1.0 / ac_len
    bx, by = bc_x * inv_bc, cy * inv_bc
    ax, ay = cx * inv_ac, cy * inv_ac
    return [*e1, -dot3(e1, a), *e2, -dot3(e2, a), *n, -dot3(n, a),
            ab_len, bx, by, bx * ab_len, by * ab_len, bc_len, ax, ay, ac_len]


def facet_square(p, k):
    px, py, pz = p
    u = px * k[0] + py * k[1] + (pz * k[2] + k[3])
    v = px * k[4] + py * k[5] + (pz * k[6] + k[7])
    h = px * k[8] + py * k[9] + (pz * k[10] + k[11])
    ab, bx, by, bxl, byl, bc, ax, ay, ac = k[12:21]
    r1 = u - jnp.clip(u, 0.0, ab)
    t2 = bx * u + by * v - bxl
    s2 = bx * v - by * u + byl
    r2 = t2 - jnp.clip(t2, 0.0, bc)
    t3 = ax * u + ay * v
    s3 = ay * u - ax * v
    r3 = t3 - jnp.clip(t3, 0.0, ac)
    edge = jnp.minimum(jnp.minimum(r1 * r1 + v * v, r2 * r2 + s2 * s2), r3 * r3 + s3 * s3)
    inside = jnp.minimum(jnp.minimum(v, s2), s3) >= 0.0
    return h * h + jnp.where(inside, 0.0, edge)


def as_columns(row):
    return jnp.transpose(jnp.broadcast_to(row, (LANES, LANES)))


def compute_kernel(cand_ref, table, moments, vol_ref, flag_ref, disp_ref, wall_ref,
                   cols, acc, moved, index, const, best):
    surf = lax.axis_index("surf")

    def one_block(block, carry):
        row = surf * 4 + block
        lanes = pl.ds(pl.multiple_of(row * LANES, LANES), LANES)
        rows = [vol_ref[pl.ds(c, 1), lanes] for c in range(3)]
        for c in range(3):
            cols[c] = as_columns(rows[c])
        count = jnp.int32(0)
        for j in range(16):
            count += (cand_ref[row, j] >= 0).astype(jnp.int32)

        def add_terms(carry, d, s):
            q = d[0] * d[0] + d[1] * d[1] + d[2] * d[2] + smoothing
            inv = 1.0 / q
            return inv * inv

        center = []
        for x in range(NX):
            ids = leaf_ids(x)
            listed = ids == cand_ref[row, 0]
            for j in range(1, 16):
                listed = listed | (ids == cand_ref[row, j])
            center.append(jnp.where(listed, 0.0, float(LEAF)))
        for g in range(LANES // PG):
            part = pl.ds(g * PG, PG)
            p = [cols[c, part, :] for c in range(3)]
            sums = [jnp.zeros((PG, LANES), jnp.float32) for _ in range(4)]
            for x in range(NX):
                m = moments[x]
                d = [m[c:c + 1] - p[c] for c in range(3)]
                w = add_terms(None, d, None) * center[x]
                for c in range(3):
                    sums[c] = sums[c] + w * m[3 + c:4 + c]
                sums[3] = sums[3] + w

            def near(j, sums):
                p0, p1, _ = leaf_places(cand_ref[row, j])
                sums = list(sums)
                for half in range(2):
                    def at(part_, place_, r):
                        return table[part_, place_, pl.ds(r + half, 1), :]
                    d = [at(0, p0, 2 * c) - p[c] for c in range(3)]
                    w = add_terms(None, d, None)
                    shift = [at(0, p0, 6), at(1, p1, 0), at(1, p1, 2)]
                    for c in range(3):
                        sums[c] = sums[c] + w * shift[c]
                    sums[3] = sums[3] + w
                return tuple(sums)

            sums = lax.fori_loop(0, count, near, tuple(sums))
            for c in range(4):
                acc[c, part, :] = sums[c]
        total = [jnp.sum(jnp.transpose(acc[c]), axis=0, keepdims=True) for c in range(4)]
        inv = 1.0 / total[3]
        out_lanes = pl.ds(pl.multiple_of(block * LANES, LANES), LANES)
        for c in range(3):
            disp = total[c] * inv
            disp_ref[pl.ds(c, 1), out_lanes] = disp
            cols[c] = as_columns(rows[c] + disp)
        flags = flag_ref[pl.ds(row, 1), :]
        flagged = jnp.max(flags) > 0
        wall_ref[pl.ds(block, 1), :] = jnp.zeros((1, LANES), jnp.float32)

        @pl.when(flagged)
        def _():
            def fetch(j, carry):
                p0, p1, p2 = leaf_places(jnp.maximum(cand_ref[row, j], 0))
                here = pl.ds(j, 1)
                for half in range(2):
                    s = [table[0, p0, pl.ds(6 + half, 1), :], table[1, p1, pl.ds(half, 1), :],
                         table[1, p1, pl.ds(2 + half, 1), :]]
                    for c in range(3):
                        moved[c, half, here, :] = table[0, p0, pl.ds(2 * c + half, 1), :] + s[c]
                for quarter in range(4):
                    index[0, quarter, here, :] = table[1, p1, pl.ds(4 + quarter, 1), :].astype(jnp.int32)
                    index[1, quarter, here, :] = table[2, p2, pl.ds(quarter, 1), :].astype(jnp.int32)
                    index[2, quarter, here, :] = table[2, p2, pl.ds(4 + quarter, 1), :].astype(jnp.int32)
                return carry

            lax.fori_loop(0, 16, fetch, 0)
            for quarter in range(4):
                corners = []
                for k in range(3):
                    where = index[k, quarter]
                    low = where % LANES
                    corner = []
                    for c in range(3):
                        lo = jnp.take_along_axis(moved[c, 0], low, axis=1, mode="promise_in_bounds")
                        hi = jnp.take_along_axis(moved[c, 1], low, axis=1, mode="promise_in_bounds")
                        corner.append(jnp.where(where < LANES, lo, hi))
                    corners.append(corner)
                for i, value in enumerate(facet_constants(*corners)):
                    const[i, quarter] = value
            best[...] = jnp.full((LANES, LANES), big_value, jnp.float32)

            def one_leaf(j, carry):
                for quarter in range(4):
                    k = [jnp.broadcast_to(const[i, quarter, pl.ds(j, 1), :], (8, LANES)) for i in range(21)]
                    for g in range(16):
                        part = pl.ds(g * 8, 8)
                        p = [cols[c, part, :] for c in range(3)]
                        best[part, :] = jnp.minimum(best[part, :], facet_square(p, k))
                return carry

            lax.fori_loop(0, count, one_leaf, 0)
            nearest = jnp.min(jnp.transpose(best[...]), axis=0, keepdims=True)
            wall_ref[pl.ds(block, 1), :] = jnp.where(flags == 1, jnp.sqrt(nearest), 0.0)

        return carry

    lax.fori_loop(0, 4, one_block, 0)


def compute(candidates, table, moments, points, flags):
    f32 = jnp.float32
    vmem = pl.BlockSpec(memory_space=pltpu.VMEM)
    return pl.pallas_call(
        compute_kernel,
        out_shape=(
            jax.ShapeDtypeStruct((3, 4 * LANES), f32),
            jax.ShapeDtypeStruct((4, LANES), f32),
        ),
        in_specs=[pl.BlockSpec(memory_space=pltpu.SMEM), vmem, vmem, vmem, vmem],
        out_specs=(vmem, vmem),
        scratch_shapes=[
            pltpu.VMEM((3, LANES, LANES), f32),
            pltpu.VMEM((4, LANES, LANES), f32),
            pltpu.VMEM((3, 2, 16, LANES), f32),
            pltpu.VMEM((3, 4, 16, LANES), jnp.int32),
            pltpu.VMEM((21, 4, 16, LANES), f32),
            pltpu.VMEM((LANES, LANES), f32),
        ],
        compiler_params=pltpu.CompilerParams(vmem_limit_bytes=40 * 2**20),
    )(candidates, table, moments, points, flags)


def body(surface_points, surface_shift, facet_nodes, volume_points, near_wall, candidates):
    table, moments = gather(surface_points, surface_shift, facet_nodes)
    flags = near_wall.reshape(-1, LANES)
    displacement, wall = compute(candidates, table, moments, volume_points, flags)
    return displacement, wall.reshape(-1)


def solution(mesh):
    placed = (
        P(None, ("vol", "surf")),
        P(None, ("vol", "surf")),
        P(("vol", "surf"), None, None),
        P(None, "vol"),
        P("vol"),
        P("vol", None),
    )
    return jax.shard_map(
        body,
        mesh=mesh,
        in_specs=placed,
        out_specs=(P(None, ("vol", "surf")), P(("vol", "surf"))),
        check_vma=False,
    )
```

time: 1620 us -> 103 us (0.06)
  the two profiles are of different devices: /device:TPU:99 before, /device:TPU:120 now
where the time goes in v1:
time: 103 us; the launch traced here: 102 us
  Pallas kernels  91.8 us (89%)
  local copies, waits for them, and re-layouts  9.98 us (10%)
    pallas_call x1, Pallas kernels, compute(): pl.pallas_call(compute_kernel, out_shape=(jax.ShapeDtypeStruct((3, 4 * LA...  49.4 us
    pallas_call x1, Pallas kernels, gather(): pl.pallas_call(gather_kernel, out_shape=(jax.ShapeDtypeStruct((3, LEAVES,...  42.4 us
    unnamed x14, local copies, waits for them, and re-layouts  9.98 us

profile of v1, /device:TPU:120, one launch (start us, length us, event | category | flops | bytes accessed | tf_op | source)
XLA Modules:
  0.0 102.4 jit_solution(5528595458321751408)
XLA Ops:
  0.6 0.7 copy.8.facets_ref
  1.3 0.0 copy-start.4
  1.3 0.7 copy-done.4
  2.0 0.0 copy-start.5
  2.0 0.7 copy-done.5
  2.7 42.4 %shard_map.77 = (f32[3,512,8,128]{3,2,1,0:T(8,128)S(1)}, f32[4,8,128]{2,1,0:T(8,128)S(1)}) custom-call(f32[3,512]{1,0:T(4,128)S(1)} %copy-done.4, f32[3,512]{1,0:T(4,128)S(1)} %copy-done.5, s32[2,3,512]{2,1,0:T(4,128)S(1)} %copy.8.facets_ref), custom_call_target="tpu_custom_call" | custom-call | tf_op jit(solution)/shard_map/pallas_call | solution.py:233
  45.1 0.0 copy-start
  45.1 2.6 %copy-done = f32[3,512,8,128]{3,2,1,0:T(8,128)} copy-done((f32[3,512,8,128]{3,2,1,0:T(8,128)}, f32[3,512,8,128]{3,2,1,0:T(8,128)S(1)}, u32[]{:S(2)}) %copy-start) | copy-done | bytes 6291480
  47.8 0.8 copy.9.cand_ref
  48.6 0.0 copy-start.1
  48.6 2.8 %copy-done.1 = f32[3,512,8,128]{3,2,1,0:T(8,128)S(1)} copy-done((f32[3,512,8,128]{3,2,1,0:T(8,128)S(1)}, f32[3,512,8,128]{3,2,1,0:T(8,128)}, u32[]{:S(2)}) %copy-start.1) | copy-done | bytes 6291480
  51.3 0.0 copy-start.2
  51.3 0.9 copy-done.2
  52.2 0.0 copy-start.3
  52.2 0.8 copy-done.3
  53.0 49.4 %shard_map.78 = (f32[3,512]{1,0:T(4,128)}, f32[4,128]{1,0:T(4,128)}) custom-call(s32[64,16]{1,0:T(8,128)S(1)} %copy.9.cand_ref, f32[3,512,8,128]{3,2,1,0:T(8,128)S(1)} %copy-done.1, f32[4,8,128]{2,1,0:T(8,128)S(1)} %get-tuple-element.7.moments, f32[3,8192]{1,0:T(4,128)S(1)} %copy-done.2, s32[64,128]{1,0:T(8,128)S(1)} %bitcast.2), custom_call_target="tpu_custom_call" | custom-call | tf_op jit(solution)/shard_map/pallas_call | solution.py:451
Async XLA Ops:
  1.3 0.7 copy-start.4
  2.0 0.7 copy-start.5
  45.1 2.7 %copy-start = (f32[3,512,8,128]{3,2,1,0:T(8,128)}, f32[3,512,8,128]{3,2,1,0:T(8,128)S(1)}, u32[]{:S(2)}) copy-start(f32[3,512,8,128]{3,2,1,0:T(8,128)S(1)} %get-tuple-element.6.table) | copy-start | bytes 18874372
  48.6 2.8 %copy-start.1 = (f32[3,512,8,128]{3,2,1,0:T(8,128)S(1)}, f32[3,512,8,128]{3,2,1,0:T(8,128)}, u32[]{:S(2)}) copy-start(f32[3,512,8,128]{3,2,1,0:T(8,128)} %copy-done) | copy-start | bytes 18874372
  51.3 0.9 copy-start.2
  52.2 0.8 copy-start.3

commit v2 on v1

--- a/solution.py
+++ b/solution.py
@@ -283,6 +283,7 @@
     return (vol * 16 + z * 2 + y % 2) * 2 + lane % 2
 
 
+margin = 1e-4
 PG = 32
 CONST = 20
 
@@ -387,10 +388,12 @@
         total = [jnp.sum(jnp.transpose(acc[c]), axis=0, keepdims=True) for c in range(4)]
         inv = 1.0 / total[3]
         out_lanes = pl.ds(pl.multiple_of(block * LANES, LANES), LANES)
+        targets = []
         for c in range(3):
             disp = total[c] * inv
             disp_ref[pl.ds(c, 1), out_lanes] = disp
-            cols[c] = as_columns(rows[c] + disp)
+            targets.append(rows[c] + disp)
+            cols[c] = as_columns(targets[c])
         flags = flag_ref[pl.ds(row, 1), :]
         flagged = jnp.max(flags) > 0
         wall_ref[pl.ds(block, 1), :] = jnp.zeros((1, LANES), jnp.float32)
@@ -427,18 +430,67 @@
                     const[i, quarter] = value
             best[...] = jnp.full((LANES, LANES), big_value, jnp.float32)
 
-            def one_leaf(j, carry):
+            def one_leaf(j):
                 for quarter in range(4):
                     k = [jnp.broadcast_to(const[i, quarter, pl.ds(j, 1), :], (8, LANES)) for i in range(21)]
                     for g in range(16):
                         part = pl.ds(g * 8, 8)
                         p = [cols[c, part, :] for c in range(3)]
                         best[part, :] = jnp.minimum(best[part, :], facet_square(p, k))
-                return carry
-
-            lax.fori_loop(0, count, one_leaf, 0)
-            nearest = jnp.min(jnp.transpose(best[...]), axis=0, keepdims=True)
-            wall_ref[pl.ds(block, 1), :] = jnp.where(flags == 1, jnp.sqrt(nearest), 0.0)
+
+            slot = lax.broadcasted_iota(jnp.int32, (16, 1), 0)
+            middle = [
+                jnp.sum(moved[c, 0] + moved[c, 1], axis=1, keepdims=True) * (1.0 / LEAF) for c in range(3)
+            ]
+            spread = [
+                sum((moved[c, half] - middle[c]) * (moved[c, half] - middle[c]) for c in range(3))
+                for half in range(2)
+            ]
+            radius = jnp.sqrt(jnp.max(jnp.maximum(*spread), axis=1, keepdims=True)) + margin
+            away = [middle[c] - targets[c] for c in range(3)]
+            away = jnp.sqrt(dot3(away, away))
+            valid = slot < count
+            lower = jnp.maximum(away - radius, 0.0)
+            lower = jnp.where(valid & (flags == 1), lower * lower, big_value)
+            upper = jnp.where(valid, away + radius, 1e15)
+            upper = jnp.min(upper * upper, axis=0, keepdims=True)
+            rank = jnp.sum(jnp.where(flags == 1, away, 0.0), axis=1, keepdims=True)
+            rank = jnp.where(valid, rank, big_value)
+
+            def nearest_slot(rank):
+                low = jnp.min(rank, axis=0, keepdims=True)
+                return jnp.min(jnp.where(rank == low, slot, 15))
+
+            def so_far():
+                return jnp.min(jnp.transpose(best[...]), axis=0, keepdims=True)
+
+            def wanted(open_):
+                below = lower < jnp.minimum(so_far(), upper)
+                hit = jnp.max(jnp.where(below, 1.0, 0.0), axis=1, keepdims=True)
+                return jnp.where(open_, hit, 0.0)
+
+            first = nearest_slot(rank)
+            one_leaf(first)
+            open_ = slot != first
+            hit = wanted(open_)
+
+            @pl.when(jnp.max(hit) > 0.0)
+            def _():
+                second = nearest_slot(jnp.where(hit > 0.0, rank, big_value))
+                one_leaf(second)
+                rest = wanted(open_ & (slot != second))
+                bits = jnp.sum(jnp.where(rest > 0.0, lax.shift_left(jnp.ones_like(slot), slot), 0))
+
+                def perhaps(j, carry):
+                    @pl.when(lax.shift_right_logical(bits, j) % 2 == 1)
+                    def _():
+                        one_leaf(j)
+
+                    return carry
+
+                lax.fori_loop(0, count, perhaps, 0)
+
+            wall_ref[pl.ds(block, 1), :] = jnp.where(flags == 1, jnp.sqrt(so_far()), 0.0)
 
         return carry
 

time: 103 us -> 90.2 us (0.88)
  the two profiles are of different devices: /device:TPU:120 before, /device:TPU:39 now
where the time goes in v2:
time: 90.2 us; the launch traced here: 89.8 us
  Pallas kernels  79.2 us (88%)
  local copies, waits for them, and re-layouts  9.98 us (11%)
    pallas_call x1, Pallas kernels, gather(): pl.pallas_call(gather_kernel, out_shape=(jax.ShapeDtypeStruct((3, LEAVES,...  43.8 us
    pallas_call x1, Pallas kernels, compute(): pl.pallas_call(compute_kernel, out_shape=(jax.ShapeDtypeStruct((3, 4 * LA...  35.4 us
    unnamed x14, local copies, waits for them, and re-layouts  9.98 us

profile of v2, /device:TPU:39, one launch (start us, length us, event | category | flops | bytes accessed | tf_op | source)
XLA Modules:
  0.0 89.8 jit_solution(13821839409553173474)
XLA Ops:
  0.6 0.7 copy.8.facets_ref
  1.3 0.0 copy-start.4
  1.3 0.7 copy-done.4
  2.0 0.0 copy-start.5
  2.0 0.7 copy-done.5
  2.7 43.8 %shard_map.77 = (f32[3,512,8,128]{3,2,1,0:T(8,128)S(1)}, f32[4,8,128]{2,1,0:T(8,128)S(1)}) custom-call(f32[3,512]{1,0:T(4,128)S(1)} %copy-done.4, f32[3,512]{1,0:T(4,128)S(1)} %copy-done.5, s32[2,3,512]{2,1,0:T(4,128)S(1)} %copy.8.facets_ref), custom_call_target="tpu_custom_call" | custom-call | tf_op jit(solution)/shard_map/pallas_call | solution.py:233
  46.5 0.0 copy-start
  46.5 2.6 %copy-done = f32[3,512,8,128]{3,2,1,0:T(8,128)} copy-done((f32[3,512,8,128]{3,2,1,0:T(8,128)}, f32[3,512,8,128]{3,2,1,0:T(8,128)S(1)}, u32[]{:S(2)}) %copy-start) | copy-done | bytes 6291480
  49.2 0.8 copy.9.cand_ref
  49.9 0.0 copy-start.1
  49.9 2.8 %copy-done.1 = f32[3,512,8,128]{3,2,1,0:T(8,128)S(1)} copy-done((f32[3,512,8,128]{3,2,1,0:T(8,128)S(1)}, f32[3,512,8,128]{3,2,1,0:T(8,128)}, u32[]{:S(2)}) %copy-start.1) | copy-done | bytes 6291480
  52.7 0.0 copy-start.2
  52.7 0.9 %copy-done.2 = f32[3,8192]{1,0:T(4,128)S(1)} copy-done((f32[3,8192]{1,0:T(4,128)S(1)}, f32[3,8192]{1,0:T(4,128)}, u32[]{:S(2)}) %copy-start.2) | copy-done | bytes 98328
  53.6 0.0 copy-start.3
  53.6 0.8 copy-done.3
  54.4 35.4 %shard_map.78 = (f32[3,512]{1,0:T(4,128)}, f32[4,128]{1,0:T(4,128)}) custom-call(s32[64,16]{1,0:T(8,128)S(1)} %copy.9.cand_ref, f32[3,512,8,128]{3,2,1,0:T(8,128)S(1)} %copy-done.1, f32[4,8,128]{2,1,0:T(8,128)S(1)} %get-tuple-element.7.moments, f32[3,8192]{1,0:T(4,128)S(1)} %copy-done.2, s32[64,128]{1,0:T(8,128)S(1)} %bitcast.2), custom_call_target="tpu_custom_call" | custom-call | tf_op jit(solution)/shard_map/pallas_call | solution.py:503
Async XLA Ops:
  1.3 0.7 copy-start.4
  2.0 0.7 copy-start.5
  46.5 2.7 %copy-start = (f32[3,512,8,128]{3,2,1,0:T(8,128)}, f32[3,512,8,128]{3,2,1,0:T(8,128)S(1)}, u32[]{:S(2)}) copy-start(f32[3,512,8,128]{3,2,1,0:T(8,128)S(1)} %get-tuple-element.6.table) | copy-start | bytes 18874372
  49.9 2.8 %copy-start.1 = (f32[3,512,8,128]{3,2,1,0:T(8,128)S(1)}, f32[3,512,8,128]{3,2,1,0:T(8,128)}, u32[]{:S(2)}) copy-start(f32[3,512,8,128]{3,2,1,0:T(8,128)} %copy-done) | copy-start | bytes 18874372
  52.7 0.9 %copy-start.2 = (f32[3,8192]{1,0:T(4,128)S(1)}, f32[3,8192]{1,0:T(4,128)}, u32[]{:S(2)}) copy-start(f32[3,8192]{1,0:T(4,128)} %vol_ref.1) | copy-start | bytes 294916
  53.6 0.8 copy-start.3

commit v3 on v2

v3 whole, which is shorter than its diff:
```python
import jax
import jax.numpy as jnp
from jax import lax
from jax.experimental import pallas as pl
from jax.experimental.pallas import tpu as pltpu
from jax.sharding import PartitionSpec as P

MESH = pl.DeviceIdType.MESH
smoothing = 0.01
big_value = 1e30

NX, NY, NZ = 4, 4, 8
SIZES = {"x": NX, "y": NY, "z": NZ}
LEAF = 256
CHIPS = NX * NY * NZ
LANES = 128
ROWS = 4


def coords_of(vol, surf):
    return {
        "x": (vol // 2) % NX,
        "y": (vol // (2 * NX)) * 2 + surf % 2,
        "z": surf // 2,
        "c": vol % 2,
    }


def mesh_id(c):
    return ((c["y"] // 2) * NX + c["x"]) * 2 + c["c"], c["z"] * 2 + c["y"] % 2


def shifted(c, axis, k):
    n = SIZES[axis]
    return {**c, axis: lax.rem(c[axis] + (k % n), n)}


WAYS = (("z", "y", "x"), ("z", "x", "y"))
NEAR_FIRST = {4: (1, 3, 2), 8: (1, 7, 2, 6, 3, 5, 4)}


def span(table, part, phase, c):
    if phase == 0:
        return table.at[:, c["c"], c["x"], c["y"], pl.ds(c["z"] * 3, 3)]
    if phase == 1:
        return table.at[part, c["c"], c["x"], c["y"]]
    if part == 0:
        return table.at[0, c["c"], c["x"]]
    return table.at[1, c["c"], :, c["y"]]


def leaf_index(leaf):
    device = leaf // 2
    c = coords_of(device // 16, device % 16)
    return leaf % 2, c["c"], c["x"], c["y"], c["z"] * 3


def gather_kernel(cand_hbm, points_hbm, shift_hbm, facets_hbm, vol_hbm, listed_ref, disp_ref, target_ref,
                  nodes, facets, mom_own, mom_z, mom_y, mom_c, moments, cols, acc,
                  cand_ref, points_ref, shift_ref, facets_ref, vol_ref,
                  in_sem, send_sem, recv_sem, core_send, core_recv, mom_send, mom_recv):
    surf = lax.axis_index("surf")
    me = coords_of(lax.axis_index("vol"), surf)
    sibling = {**me, "c": 1 - me["c"]}
    partners = [sibling]
    for axis, n in SIZES.items():
        partners += [shifted(me, axis, k) for k in range(1, n)]
    barrier = pltpu.get_barrier_semaphore()
    for other in partners:
        pl.semaphore_signal(barrier, inc=1, device_id=mesh_id(other), device_id_type=MESH)
    share = pl.ds(pl.multiple_of(surf * 4 * LANES, 4 * LANES), 4 * LANES)
    inputs = [
        pltpu.make_async_copy(points_hbm, points_ref, in_sem.at[0]),
        pltpu.make_async_copy(shift_hbm, shift_ref, in_sem.at[1]),
        pltpu.make_async_copy(facets_hbm, facets_ref, in_sem.at[2]),
        pltpu.make_async_copy(vol_hbm.at[:, share], vol_ref, in_sem.at[3]),
        pltpu.make_async_copy(cand_hbm, cand_ref, in_sem.at[4]),
    ]
    for copy in inputs:
        copy.start()
    for copy in inputs:
        copy.wait()

    for leaf in range(2):
        own = (leaf, me["c"], me["x"], me["y"])
        for half in range(2):
            lanes = pl.ds(leaf * LEAF + half * LANES, LANES)
            for c in range(3):
                nodes[(*own, me["z"] * 3 + (2 * c) // 4, pl.ds((2 * c) % 4 + half, 1), slice(None))] = (
                    points_ref[pl.ds(c, 1), lanes]
                )
                nodes[(*own, me["z"] * 3 + (6 + 2 * c) // 4, pl.ds((6 + 2 * c) % 4 + half, 1), slice(None))] = (
                    shift_ref[pl.ds(c, 1), lanes]
                )
        for quarter in range(4):
            lanes = pl.ds(quarter * LANES, LANES)
            for k in range(3):
                facets[(*own, me["z"] * 3 + k, pl.ds(quarter, 1), slice(None))] = (
                    facets_ref[k, pl.ds(leaf, 1), lanes].astype(jnp.float32)
                )
    lane = lax.broadcasted_iota(jnp.int32, (3, LANES), 1)
    my_lane = ((me["c"] * NY + me["y"]) * NZ + me["z"]) * 2
    for row, ref in ((0, points_ref), (3, shift_ref)):
        tile = jnp.zeros((3, LANES), jnp.float32)
        for leaf in range(2):
            mean = jnp.sum(ref[:, pl.ds(leaf * LEAF, LEAF)], axis=1, keepdims=True) * (1.0 / LEAF)
            tile = jnp.where(lane == my_lane + leaf, mean, tile)
        mom_own[pl.ds(row, 3), :] = tile
    mom_own[pl.ds(6, 2), :] = jnp.zeros((2, LANES), jnp.float32)
    pl.semaphore_wait(barrier, len(partners))

    sent = []

    def remote(src, dst, to, s_sem, r_sem):
        return pltpu.make_async_remote_copy(
            src_ref=src, dst_ref=dst, send_sem=s_sem, recv_sem=r_sem,
            device_id=mesh_id(to), device_id_type=MESH,
        )

    def start(copy):
        copy.start()
        sent.append(copy)

    tables = (nodes, facets)

    def sems(which, part, phase, k):
        slot = (part, phase, k)
        return send_sem.at[(which, *slot)], recv_sem.at[(which, *slot)]

    def issue(which, part, phase):
        axis = WAYS[part][phase]
        mine = span(tables[which], part, phase, me)
        for k in NEAR_FIRST[SIZES[axis]]:
            start(remote(mine, mine, shifted(me, axis, k), *sems(which, part, phase, k)))

    def collect(which, part, phase, steps=None):
        axis = WAYS[part][phase]
        for k in steps or NEAR_FIRST[SIZES[axis]]:
            frm = shifted(me, axis, -k)
            theirs = span(tables[which], part, phase, frm)
            remote(theirs, theirs, frm, *sems(which, part, phase, k)).wait_recv()

    def to_sibling(which, part, k):
        mine = span(tables[which], part, 2, shifted(me, WAYS[part][2], -k))
        start(remote(mine, mine, sibling, core_send.at[which, part, k], core_recv.at[which, part, k]))

    def from_sibling(which, part, k):
        theirs = span(tables[which], part, 2, shifted(sibling, WAYS[part][2], -k))
        remote(theirs, theirs, sibling, core_send.at[which, part, k], core_recv.at[which, part, k]).wait_recv()

    def mom_copies(dst, others, slot0):
        return [
            remote(mom_own, dst.at[k], other, mom_send.at[slot0 + k], mom_recv.at[slot0 + k])
            for k, other in enumerate(others)
        ]

    def mom_sum(copies, arrived):
        total = mom_own[...]
        for k, copy in enumerate(copies):
            copy.wait()
            total = total + arrived[k]
        mom_own[...] = total

    issue(0, 0, 0)
    mom = mom_copies(mom_z, [shifted(me, "z", k) for k in range(1, NZ)], 0)
    for copy in mom:
        copy.start()
    issue(1, 0, 0)
    collect(0, 0, 0)
    issue(0, 0, 1)
    issue(0, 1, 1)
    mom_sum(mom, mom_z)
    mom = mom_copies(mom_y, [shifted(me, "y", k) for k in range(1, NY)], 7)
    for copy in mom:
        copy.start()
    collect(1, 0, 0)
    issue(1, 0, 1)
    issue(1, 1, 1)
    for part in range(2):
        collect(0, part, 1)
        issue(0, part, 2)
    for part in range(2):
        to_sibling(0, part, 0)
    mom_sum(mom, mom_y)
    mom = mom_copies(mom_c, [sibling], 10)
    mom[0].start()
    for part in range(2):
        collect(1, part, 1)
    mom_sum(mom, mom_c)
    moments[pl.ds(me["x"], 1)] = mom_own[...][None]
    for k in range(1, NX):
        start(remote(mom_own, moments.at[me["x"]], shifted(me, "x", k), mom_send.at[10 + k], mom_recv.at[10 + k]))
    for k in (1, 3, 2):
        for part in range(2):
            collect(0, part, 2, (k,))
            to_sibling(0, part, k)
    for part in range(2):
        issue(1, part, 2)
        to_sibling(1, part, 0)
    for k in range(1, NX):
        frm = shifted(me, "x", -k)
        remote(mom_own, moments.at[frm["x"]], frm, mom_send.at[10 + k], mom_recv.at[10 + k]).wait_recv()
    for part in range(2):
        for k in range(4):
            from_sibling(0, part, k)

    def displace(block):
        row = surf * 4 + block
        out_lanes = pl.ds(block * LANES, LANES)
        rows = [vol_ref[pl.ds(c, 1), out_lanes] for c in range(3)]
        for c in range(3):
            cols[c] = as_columns(rows[c])
        centers = []
        for x in range(NX):
            ids = leaf_ids(x)
            listed = ids == cand_ref[0, row]
            for j in range(1, 16):
                listed = listed | (ids == cand_ref[j, row])
            centers.append(jnp.where(listed, 0.0, float(LEAF)))

        def point_group(g, carry):
            part = pl.ds(pl.multiple_of(g * PG, PG), PG)
            p = [cols[c, part, :] for c in range(3)]
            sums = [jnp.zeros((PG, LANES), jnp.float32) for _ in range(4)]
            for x in range(NX):
                m = moments[x]
                w = weight([m[c:c + 1] - p[c] for c in range(3)]) * centers[x]
                for c in range(3):
                    sums[c] = sums[c] + w * m[3 + c:4 + c]
                sums[3] = sums[3] + w

            def near(j, sums):
                leaf = cand_ref[j, row]
                real = jnp.where(leaf >= 0, 1.0, 0.0)
                i0, i1, i2, i3, quad = leaf_index(jnp.maximum(leaf, 0))
                sums = list(sums)
                for half in range(2):
                    at = [nodes[i0, i1, i2, i3, quad + (2 * c) // 4, pl.ds((2 * c) % 4 + half, 1), :] for c in range(6)]
                    w = weight([at[c] - p[c] for c in range(3)]) * real
                    for c in range(3):
                        sums[c] = sums[c] + w * at[3 + c]
                    sums[3] = sums[3] + w
                return tuple(sums)

            sums = lax.fori_loop(0, 16, near, tuple(sums))
            for c in range(4):
                acc[c, part, :] = sums[c]
            return carry

        lax.fori_loop(0, LANES // PG, point_group, 0)
        total = [jnp.sum(jnp.transpose(acc[c]), axis=0, keepdims=True) for c in range(4)]
        inv = 1.0 / total[3]
        for c in range(3):
            disp = total[c] * inv
            disp_ref[pl.ds(c, 1), out_lanes] = disp
            target_ref[pl.ds(c, 1), out_lanes] = rows[c] + disp

    displace(0)
    displace(1)
    for k in (1, 3):
        for part in range(2):
            collect(1, part, 2, (k,))
            to_sibling(1, part, k)
    displace(2)
    for part in range(2):
        collect(1, part, 2, (2,))
        to_sibling(1, part, 2)
    displace(3)
    for part in range(2):
        for k in range(4):
            from_sibling(1, part, k)

    def hand_out(n, carry):
        leaf = jnp.maximum(cand_ref[n % 16, surf * 4 + n // 16], 0)
        i0, i1, i2, i3, quad = leaf_index(leaf)
        for q in range(3):
            listed_ref[n, q] = nodes[i0, i1, i2, i3, quad + q]
            listed_ref[n, 3 + q] = facets[i0, i1, i2, i3, quad + q]
        return carry

    lax.fori_loop(0, 64, hand_out, 0)
    for copy in sent:
        copy.wait_send()


def displace_and_list(candidates, points, shift, facets, vol):
    f32 = jnp.float32
    vmem = pl.BlockSpec(memory_space=pltpu.VMEM)
    table = pltpu.VMEM((2, 2, NX, NY, NZ * 3, ROWS, LANES), f32)
    dma = pltpu.SemaphoreType.DMA
    return pl.pallas_call(
        gather_kernel,
        name="displace",
        out_shape=(
            jax.ShapeDtypeStruct((64, 6, ROWS, LANES), f32),
            jax.ShapeDtypeStruct((3, 4 * LANES), f32),
            jax.ShapeDtypeStruct((3, 4 * LANES), f32),
        ),
        in_specs=[pl.BlockSpec(memory_space=pltpu.HBM)] * 5,
        out_specs=(vmem, vmem, vmem),
        scratch_shapes=[
            table,
            table,
            pltpu.VMEM((8, LANES), f32),
            pltpu.VMEM((7, 8, LANES), f32),
            pltpu.VMEM((3, 8, LANES), f32),
            pltpu.VMEM((1, 8, LANES), f32),
            pltpu.VMEM((NX, 8, LANES), f32),
            pltpu.VMEM((3, LANES, LANES), f32),
            pltpu.VMEM((4, LANES, LANES), f32),
            pltpu.SMEM((16, 64), jnp.int32),
            pltpu.VMEM((3, 4 * LANES), f32),
            pltpu.VMEM((3, 4 * LANES), f32),
            pltpu.VMEM((3, 2, 4 * LANES), jnp.int32),
            pltpu.VMEM((3, 4 * LANES), f32),
            dma((5,)),
            dma((2, 2, 3, 8)),
            dma((2, 2, 3, 8)),
            dma((2, 2, 4)),
            dma((2, 2, 4)),
            dma((14,)),
            dma((14,)),
        ],
        compiler_params=pltpu.CompilerParams(
            collective_id=0, has_side_effects=True, vmem_limit_bytes=24 * 2**20
        ),
    )(candidates, points, shift, facets, vol)


def dot3(a, b):
    return a[0] * b[0] + a[1] * b[1] + a[2] * b[2]


def minus3(a, b):
    return [a[0] - b[0], a[1] - b[1], a[2] - b[2]]


def cross3(a, b):
    return [a[1] * b[2] - a[2] * b[1], a[2] * b[0] - a[0] * b[2], a[0] * b[1] - a[1] * b[0]]


def leaf_ids(x):
    lane = lax.broadcasted_iota(jnp.int32, (1, LANES), 1)
    z = (lane // 2) % NZ
    y = (lane // (2 * NZ)) % NY
    core = lane // (2 * NZ * NY)
    vol = ((y // 2) * NX + x) * 2 + core
    return (vol * 16 + z * 2 + y % 2) * 2 + lane % 2


margin = 1e-4
PG = 32


def facet_constants(a, b, c):
    ab, ac = minus3(b, a), minus3(c, a)
    normal = cross3(ab, ac)
    ab_len = jnp.sqrt(dot3(ab, ab))
    inv_ab = 1.0 / ab_len
    inv_n = lax.rsqrt(dot3(normal, normal))
    e1 = [q * inv_ab for q in ab]
    n = [q * inv_n for q in normal]
    e2 = cross3(n, e1)
    cx, cy = dot3(ac, e1), dot3(ac, e2)
    bc_x = cx - ab_len
    bc_len = jnp.sqrt(bc_x * bc_x + cy * cy)
    ac_len = jnp.sqrt(cx * cx + cy * cy)
    inv_bc, inv_ac = 1.0 / bc_len, 1.0 / ac_len
    bx, by = bc_x * inv_bc, cy * inv_bc
    ax, ay = cx * inv_ac, cy * inv_ac
    return [*e1, -dot3(e1, a), *e2, -dot3(e2, a), *n, -dot3(n, a),
            ab_len, bx, by, bx * ab_len, by * ab_len, bc_len, ax, ay, ac_len]


def facet_square(p, k):
    px, py, pz = p
    u = px * k[0] + py * k[1] + (pz * k[2] + k[3])
    v = px * k[4] + py * k[5] + (pz * k[6] + k[7])
    h = px * k[8] + py * k[9] + (pz * k[10] + k[11])
    ab, bx, by, bxl, byl, bc, ax, ay, ac = k[12:21]
    r1 = u - jnp.clip(u, 0.0, ab)
    t2 = bx * u + by * v - bxl
    s2 = bx * v - by * u + byl
    r2 = t2 - jnp.clip(t2, 0.0, bc)
    t3 = ax * u + ay * v
    s3 = ay * u - ax * v
    r3 = t3 - jnp.clip(t3, 0.0, ac)
    edge = jnp.minimum(jnp.minimum(r1 * r1 + v * v, r2 * r2 + s2 * s2), r3 * r3 + s3 * s3)
    inside = jnp.minimum(jnp.minimum(v, s2), s3) >= 0.0
    return h * h + jnp.where(inside, 0.0, edge)


def weight(d):
    inv = 1.0 / (dot3(d, d) + smoothing)
    return inv * inv


def as_columns(row):
    return jnp.transpose(jnp.broadcast_to(row, (LANES, LANES)))


def wall_kernel(cand_hbm, listed_ref, disp_in, target_ref, flag_ref, disp_ref, wall_ref,
                cols, moved, index, const, best, cand_ref, in_sem):
    surf = lax.axis_index("surf")
    copy = pltpu.make_async_copy(cand_hbm, cand_ref, in_sem)
    copy.start()
    disp_ref[...] = disp_in[...]
    copy.wait()

    def one_block(block, carry):
        row = surf * 4 + block
        lanes = pl.ds(pl.multiple_of(block * LANES, LANES), LANES)
        count = jnp.int32(0)
        for j in range(16):
            count += (cand_ref[j, row] >= 0).astype(jnp.int32)
        flags = flag_ref[pl.ds(row, 1), :]
        flagged = jnp.max(flags) > 0
        wall_ref[pl.ds(block, 1), :] = jnp.zeros((1, LANES), jnp.float32)

        @pl.when(flagged)
        def _():
            targets = [target_ref[pl.ds(c, 1), lanes] for c in range(3)]
            for c in range(3):
                cols[c] = as_columns(targets[c])

            def fetch(j, carry):
                here = pl.ds(j, 1)
                rows = block * 16 + j
                for half in range(2):
                    at = [listed_ref[rows, (2 * c) // 4, pl.ds((2 * c) % 4 + half, 1), :] for c in range(6)]
                    for c in range(3):
                        moved[c, half, here, :] = at[c] + at[3 + c]
                for k in range(3):
                    for quarter in range(4):
                        index[k, quarter, here, :] = listed_ref[rows, 3 + k, pl.ds(quarter, 1), :].astype(jnp.int32)
                return carry

            lax.fori_loop(0, 16, fetch, 0)
            for quarter in range(4):
                corners = []
                for k in range(3):
                    where = index[k, quarter]
                    low = where % LANES
                    corner = []
                    for c in range(3):
                        lo = jnp.take_along_axis(moved[c, 0], low, axis=1, mode="promise_in_bounds")
                        hi = jnp.take_along_axis(moved[c, 1], low, axis=1, mode="promise_in_bounds")
                        corner.append(jnp.where(where < LANES, lo, hi))
                    corners.append(corner)
                for i, value in enumerate(facet_constants(*corners)):
                    const[i, quarter] = value
            best[...] = jnp.full((LANES, LANES), big_value, jnp.float32)

            def one_leaf(j):
                for quarter in range(4):
                    k = [jnp.broadcast_to(const[i, quarter, pl.ds(j, 1), :], (8, LANES)) for i in range(21)]
                    for g in range(16):
                        part = pl.ds(g * 8, 8)
                        p = [cols[c, part, :] for c in range(3)]
                        best[part, :] = jnp.minimum(best[part, :], facet_square(p, k))

            slot = lax.broadcasted_iota(jnp.int32, (16, 1), 0)
            middle = [
                jnp.sum(moved[c, 0] + moved[c, 1], axis=1, keepdims=True) * (1.0 / LEAF) for c in range(3)
            ]
            spread = [
                sum((moved[c, half] - middle[c]) * (moved[c, half] - middle[c]) for c in range(3))
                for half in range(2)
            ]
            radius = jnp.sqrt(jnp.max(jnp.maximum(*spread), axis=1, keepdims=True)) + margin
            away = [middle[c] - targets[c] for c in range(3)]
            away = jnp.sqrt(dot3(away, away))
            valid = slot < count
            lower = jnp.maximum(away - radius, 0.0)
            lower = jnp.where(valid & (flags == 1), lower * lower, big_value)
            upper = jnp.where(valid, away + radius, 1e15)
            upper = jnp.min(upper * upper, axis=0, keepdims=True)
            rank = jnp.sum(jnp.where(flags == 1, away, 0.0), axis=1, keepdims=True)
            rank = jnp.where(valid, rank, big_value)

            def nearest_slot(rank):
                low = jnp.min(rank, axis=0, keepdims=True)
                return jnp.min(jnp.where(rank == low, slot, 15))

            def so_far():
                return jnp.min(jnp.transpose(best[...]), axis=0, keepdims=True)

            def wanted(open_):
                below = lower < jnp.minimum(so_far(), upper)
                hit = jnp.max(jnp.where(below, 1.0, 0.0), axis=1, keepdims=True)
                return jnp.where(open_, hit, 0.0)

            first = nearest_slot(rank)
            one_leaf(first)
            open_ = slot != first
            hit = wanted(open_)

            @pl.when(jnp.max(hit) > 0.0)
            def _():
                second = nearest_slot(jnp.where(hit > 0.0, rank, big_value))
                one_leaf(second)
                rest = wanted(open_ & (slot != second))
                bits = jnp.sum(jnp.where(rest > 0.0, lax.shift_left(jnp.ones_like(slot), slot), 0))

                def perhaps(j, carry):
                    @pl.when(lax.shift_right_logical(bits, j) % 2 == 1)
                    def _():
                        one_leaf(j)

                    return carry

                lax.fori_loop(0, count, perhaps, 0)

            wall_ref[pl.ds(block, 1), :] = jnp.where(flags == 1, jnp.sqrt(so_far()), 0.0)

        return carry

    lax.fori_loop(0, 4, one_block, 0)


def wall(candidates, listed, disp, target, flags):
    f32 = jnp.float32
    vmem = pl.BlockSpec(memory_space=pltpu.VMEM)
    return pl.pallas_call(
        wall_kernel,
        name="wall",
        out_shape=(
            jax.ShapeDtypeStruct((3, 4 * LANES), f32),
            jax.ShapeDtypeStruct((4, LANES), f32),
        ),
        in_specs=[pl.BlockSpec(memory_space=pltpu.HBM), vmem, vmem, vmem, vmem],
        out_specs=(vmem, vmem),
        scratch_shapes=[
            pltpu.VMEM((3, LANES, LANES), f32),
            pltpu.VMEM((3, 2, 16, LANES), f32),
            pltpu.VMEM((3, 4, 16, LANES), jnp.int32),
            pltpu.VMEM((21, 4, 16, LANES), f32),
            pltpu.VMEM((LANES, LANES), f32),
            pltpu.SMEM((16, 64), jnp.int32),
            pltpu.SemaphoreType.DMA,
        ],
        compiler_params=pltpu.CompilerParams(vmem_limit_bytes=24 * 2**20),
    )(candidates, listed, disp, target, flags)


def body(surface_points, surface_shift, facet_nodes, volume_points, near_wall, candidates):
    candidates = candidates.T
    listed, disp, target = displace_and_list(
        candidates, surface_points, surface_shift, jnp.transpose(facet_nodes, (1, 0, 2)), volume_points
    )
    flags = near_wall.reshape(-1, LANES)
    displacement, distance = wall(candidates, listed, disp, target, flags)
    return displacement, distance.reshape(-1)


def solution(mesh):
    placed = (
        P(None, ("vol", "surf")),
        P(None, ("vol", "surf")),
        P(("vol", "surf"), None, None),
        P(None, "vol"),
        P("vol"),
        P("vol", None),
    )
    return jax.shard_map(
        body,
        mesh=mesh,
        in_specs=placed,
        out_specs=(P(None, ("vol", "surf")), P(("vol", "surf"))),
        check_vma=False,
    )
```

time: 90.2 us -> 72.9 us (0.81)
  the two profiles are of different devices: /device:TPU:39 before, /device:TPU:42 now
where the time goes in v3:
time: 72.9 us; the launch traced here: 72.6 us
  Pallas kernels  68.2 us (94%)
  local copies, waits for them, and re-layouts  3.7 us (5%)
    pallas_call x1, Pallas kernels, displace_and_list(): pl.pallas_call(gather_kernel, name='displace', out_shape=(jax.ShapeDtypeS...  50.6 us
    pallas_call x1, Pallas kernels, wall(): pl.pallas_call(wall_kernel, name='wall', out_shape=(jax.ShapeDtypeStruct(...  17.6 us
    unnamed x12, local copies, waits for them, and re-layouts  3.7 us

profile of v3, /device:TPU:42, one launch (start us, length us, event | category | flops | bytes accessed | tf_op | source)
XLA Modules:
  0.0 72.6 jit_solution(5414209781405992666)
XLA Ops:
  0.6 0.0 copy-start
  0.6 0.9 %copy-done = f32[3,8192]{1,0:T(4,128)S(1)} copy-done((f32[3,8192]{1,0:T(4,128)S(1)}, f32[3,8192]{1,0:T(4,128)}, u32[]{:S(2)}) %copy-start) | copy-done | bytes 98328
  1.5 0.0 copy-start.1
  1.5 0.7 copy-done.1
  2.2 0.0 copy-start.3
  2.2 0.7 copy-done.3
  2.9 0.0 copy-start.4
  2.9 0.7 copy-done.4
  3.6 0.0 copy-start.5
  3.6 0.7 copy-done.5
  4.3 0.0 copy-start.2
  4.3 50.6 %displace.1 = (f32[64,6,4,128]{3,2,1,0:T(4,128)S(1)}, f32[3,512]{1,0:T(4,128)S(1)}, f32[3,512]{1,0:T(4,128)S(1)}) custom-call(s32[16,64]{1,0:T(8,128)S(1)} %bitcast.4, f32[3,512]{1,0:T(4,128)S(1)} %copy-done.4, f32[3,512]{1,0:T(4,128)S(1)} %copy-done.5, s32[3,2,512]{2,1,0:T(2,128)S(1)} %bitcast.7, f32[3,8192]{1,0:T(4,128)S(1)} %copy-done), custom_call_target="tpu_custom_call" | custom-call | tf_op jit(solution)/shard_map/displace/pallas_call | solution.py:291
  55.0 0.0 copy-done.2
  55.0 17.6 %wall.1 = (f32[3,512]{1,0:T(4,128)}, f32[4,128]{1,0:T(4,128)}) custom-call(s32[16,64]{1,0:T(8,128)S(1)} %bitcast.5, f32[64,6,4,128]{3,2,1,0:T(4,128)S(1)} %get-tuple-element.7.listed_ref, f32[3,512]{1,0:T(4,128)S(1)} %get-tuple-element.8.disp_in, f32[3,512]{1,0:T(4,128)S(1)} %get-tuple-element.9.target_ref, s32[64,128]{1,0:T(8,128)S(1)} %bitcast.6), custom_call_target="tpu_custom_call" | custom-call | tf_op jit(solution)/shard_map/wall/pallas_call | solution.py:524
Async XLA Ops:
  0.6 0.9 %copy-start = (f32[3,8192]{1,0:T(4,128)S(1)}, f32[3,8192]{1,0:T(4,128)}, u32[]{:S(2)}) copy-start(f32[3,8192]{1,0:T(4,128)} %vol_hbm.1) | copy-start | bytes 294916
  1.5 0.7 copy-start.1
  2.2 0.7 copy-start.3
  2.9 0.7 copy-start.4
  3.6 0.7 copy-start.5
  4.3 50.7 %copy-start.2 = (s32[8192]{0:T(1024)S(1)}, s32[8192]{0:T(1024)}, u32[]{:S(2)}) copy-start(s32[8192]{0:T(1024)} %param.10) | copy-start | bytes 98308

commit v4 on v3

--- a/solution.py
+++ b/solution.py
@@ -41,22 +41,29 @@
 
 def span(table, part, phase, c):
     if phase == 0:
-        return table.at[:, c["c"], c["x"], c["y"], pl.ds(c["z"] * 3, 3)]
+        return table.at[:, c["c"] * NX + c["x"], c["y"], pl.ds(c["z"] * 3, 3)]
     if phase == 1:
-        return table.at[part, c["c"], c["x"], c["y"]]
+        return table.at[part, c["c"] * NX + c["x"], c["y"]]
     if part == 0:
-        return table.at[0, c["c"], c["x"]]
-    return table.at[1, c["c"], :, c["y"]]
+        return table.at[0, c["c"] * NX + c["x"]]
+    return table.at[1, pl.ds(c["c"] * NX, NX), c["y"]]
+
+
+def half_span(table, part, c, half):
+    if part == 0:
+        return table.at[0, c["c"] * NX + c["x"], pl.ds(half * 2, 2)]
+    return table.at[1, pl.ds(c["c"] * NX + half * 2, 2), c["y"]]
 
 
 def leaf_index(leaf):
-    device = leaf // 2
-    c = coords_of(device // 16, device % 16)
-    return leaf % 2, c["c"], c["x"], c["y"], c["z"] * 3
+    right = lax.shift_right_logical
+    surf, vol = right(leaf, 1) & 15, right(leaf, 5)
+    y = (right(vol, 3) << 1) | (surf & 1)
+    return leaf & 1, ((vol & 1) << 2) | (right(vol, 1) & 3), y, right(surf, 1) * 3
 
 
 def gather_kernel(cand_hbm, points_hbm, shift_hbm, facets_hbm, vol_hbm, listed_ref, disp_ref, target_ref,
-                  nodes, facets, mom_own, mom_z, mom_y, mom_c, moments, cols, acc,
+                  nodes, facets, mom_own, mom_z, mom_y, mom_c, moments, cols, acc, where,
                   cand_ref, points_ref, shift_ref, facets_ref, vol_ref,
                   in_sem, send_sem, recv_sem, core_send, core_recv, mom_send, mom_recv):
     surf = lax.axis_index("surf")
@@ -82,7 +89,7 @@
         copy.wait()
 
     for leaf in range(2):
-        own = (leaf, me["c"], me["x"], me["y"])
+        own = (leaf, me["c"] * NX + me["x"], me["y"])
         for half in range(2):
             lanes = pl.ds(leaf * LEAF + half * LANES, LANES)
             for c in range(3):
@@ -130,7 +137,7 @@
     def issue(which, part, phase):
         axis = WAYS[part][phase]
         mine = span(tables[which], part, phase, me)
-        for k in NEAR_FIRST[SIZES[axis]]:
+        for k in (1, 3) if phase == 2 else NEAR_FIRST[SIZES[axis]]:
             start(remote(mine, mine, shifted(me, axis, k), *sems(which, part, phase, k)))
 
     def collect(which, part, phase, steps=None):
@@ -139,6 +146,17 @@
             frm = shifted(me, axis, -k)
             theirs = span(tables[which], part, phase, frm)
             remote(theirs, theirs, frm, *sems(which, part, phase, k)).wait_recv()
+
+    def forward(which, part, k):
+        axis = WAYS[part][2]
+        piece = half_span(tables[which], part, shifted(me, axis, -k), k // 2)
+        start(remote(piece, piece, shifted(me, axis, k), *sems(which, part, 2, k - 1)))
+
+    def collect_halves(which, part):
+        axis = WAYS[part][2]
+        for k in (1, 3):
+            piece = half_span(tables[which], part, shifted(me, axis, 2), k // 2)
+            remote(piece, piece, shifted(me, axis, -k), *sems(which, part, 2, k - 1)).wait_recv()
 
     def to_sibling(which, part, k):
         mine = span(tables[which], part, 2, shifted(me, WAYS[part][2], -k))
@@ -190,26 +208,22 @@
     moments[pl.ds(me["x"], 1)] = mom_own[...][None]
     for k in range(1, NX):
         start(remote(mom_own, moments.at[me["x"]], shifted(me, "x", k), mom_send.at[10 + k], mom_recv.at[10 + k]))
-    for k in (1, 3, 2):
-        for part in range(2):
-            collect(0, part, 2, (k,))
-            to_sibling(0, part, k)
-    for part in range(2):
-        issue(1, part, 2)
-        to_sibling(1, part, 0)
+    def locate(n, carry):
+        at = leaf_index(jnp.maximum(cand_ref[n % 16, surf * 4 + n // 16], 0))
+        for i in range(4):
+            where[i, n] = at[i]
+        return carry
+
+    lax.fori_loop(0, 64, locate, 0)
+    for block in range(4):
+        for c in range(3):
+            cols[block, c] = as_columns(vol_ref[pl.ds(c, 1), pl.ds(block * LANES, LANES)])
     for k in range(1, NX):
         frm = shifted(me, "x", -k)
         remote(mom_own, moments.at[frm["x"]], frm, mom_send.at[10 + k], mom_recv.at[10 + k]).wait_recv()
-    for part in range(2):
-        for k in range(4):
-            from_sibling(0, part, k)
-
-    def displace(block):
+
+    def far(block, carry):
         row = surf * 4 + block
-        out_lanes = pl.ds(block * LANES, LANES)
-        rows = [vol_ref[pl.ds(c, 1), out_lanes] for c in range(3)]
-        for c in range(3):
-            cols[c] = as_columns(rows[c])
         centers = []
         for x in range(NX):
             ids = leaf_ids(x)
@@ -217,53 +231,76 @@
             for j in range(1, 16):
                 listed = listed | (ids == cand_ref[j, row])
             centers.append(jnp.where(listed, 0.0, float(LEAF)))
-
-        def point_group(g, carry):
-            part = pl.ds(pl.multiple_of(g * PG, PG), PG)
-            p = [cols[c, part, :] for c in range(3)]
-            sums = [jnp.zeros((PG, LANES), jnp.float32) for _ in range(4)]
+        for g in range(LANES // PG):
+            part = pl.ds(g * PG, PG)
+            p = [cols[block, c, part, :] for c in range(3)]
+            sums = [None] * 4
             for x in range(NX):
                 m = moments[x]
                 w = weight([m[c:c + 1] - p[c] for c in range(3)]) * centers[x]
+                terms = [w * m[3 + c:4 + c] for c in range(3)] + [w]
+                sums = terms if x == 0 else [a + b for a, b in zip(sums, terms)]
+            for c in range(4):
+                acc[block, c, part, :] = sums[c]
+        return carry
+
+    lax.fori_loop(0, 4, far, 0)
+    for k in (1, 3):
+        for part in range(2):
+            collect(0, part, 2, (k,))
+            forward(0, part, k)
+            to_sibling(0, part, k)
+    for part in range(2):
+        issue(1, part, 2)
+    for part in range(2):
+        collect_halves(0, part)
+        to_sibling(0, part, 2)
+    for part in range(2):
+        to_sibling(1, part, 0)
+        for k in range(4):
+            from_sibling(0, part, k)
+
+    def displace(block):
+        def near(j, carry):
+            n = block * 16 + j
+            i0, i1, i2, quad = (where[i, n] for i in range(4))
+            push_off = jnp.where(cand_ref[j, surf * 4 + block] >= 0, 0.0, 1e15)
+            at = [
+                [nodes[i0, i1, i2, quad + (2 * c) // 4, pl.ds((2 * c) % 4 + half, 1), :] for c in range(6)]
+                for half in range(2)
+            ]
+            for half in range(2):
+                at[half][0] = at[half][0] + push_off
+            for g in range(LANES // PG):
+                part = pl.ds(g * PG, PG)
+                p = [cols[block, c, part, :] for c in range(3)]
+                w = [weight([at[half][c] - p[c] for c in range(3)]) for half in range(2)]
                 for c in range(3):
-                    sums[c] = sums[c] + w * m[3 + c:4 + c]
-                sums[3] = sums[3] + w
-
-            def near(j, sums):
-                leaf = cand_ref[j, row]
-                real = jnp.where(leaf >= 0, 1.0, 0.0)
-                i0, i1, i2, i3, quad = leaf_index(jnp.maximum(leaf, 0))
-                sums = list(sums)
-                for half in range(2):
-                    at = [nodes[i0, i1, i2, i3, quad + (2 * c) // 4, pl.ds((2 * c) % 4 + half, 1), :] for c in range(6)]
-                    w = weight([at[c] - p[c] for c in range(3)]) * real
-                    for c in range(3):
-                        sums[c] = sums[c] + w * at[3 + c]
-                    sums[3] = sums[3] + w
-                return tuple(sums)
-
-            sums = lax.fori_loop(0, 16, near, tuple(sums))
-            for c in range(4):
-                acc[c, part, :] = sums[c]
+                    acc[block, c, part, :] += w[0] * at[0][3 + c] + w[1] * at[1][3 + c]
+                acc[block, 3, part, :] += w[0] + w[1]
+            for q in range(3):
+                listed_ref[n, q] = nodes[i0, i1, i2, quad + q]
             return carry
 
-        lax.fori_loop(0, LANES // PG, point_group, 0)
-        total = [jnp.sum(jnp.transpose(acc[c]), axis=0, keepdims=True) for c in range(4)]
+        lax.fori_loop(0, 16, near, 0)
+        out_lanes = pl.ds(block * LANES, LANES)
+        total = [jnp.sum(jnp.transpose(acc[block, c]), axis=0, keepdims=True) for c in range(4)]
         inv = 1.0 / total[3]
         for c in range(3):
             disp = total[c] * inv
             disp_ref[pl.ds(c, 1), out_lanes] = disp
-            target_ref[pl.ds(c, 1), out_lanes] = rows[c] + disp
+            target_ref[pl.ds(c, 1), out_lanes] = vol_ref[pl.ds(c, 1), out_lanes] + disp
 
     displace(0)
-    displace(1)
     for k in (1, 3):
         for part in range(2):
             collect(1, part, 2, (k,))
+            forward(1, part, k)
             to_sibling(1, part, k)
+    displace(1)
     displace(2)
     for part in range(2):
-        collect(1, part, 2, (2,))
+        collect_halves(1, part)
         to_sibling(1, part, 2)
     displace(3)
     for part in range(2):
@@ -271,11 +308,9 @@
             from_sibling(1, part, k)
 
     def hand_out(n, carry):
-        leaf = jnp.maximum(cand_ref[n % 16, surf * 4 + n // 16], 0)
-        i0, i1, i2, i3, quad = leaf_index(leaf)
+        i0, i1, i2, quad = (where[i, n] for i in range(4))
         for q in range(3):
-            listed_ref[n, q] = nodes[i0, i1, i2, i3, quad + q]
-            listed_ref[n, 3 + q] = facets[i0, i1, i2, i3, quad + q]
+            listed_ref[n, 3 + q] = facets[i0, i1, i2, quad + q]
         return carry
 
     lax.fori_loop(0, 64, hand_out, 0)
@@ -286,7 +321,7 @@
 def displace_and_list(candidates, points, shift, facets, vol):
     f32 = jnp.float32
     vmem = pl.BlockSpec(memory_space=pltpu.VMEM)
-    table = pltpu.VMEM((2, 2, NX, NY, NZ * 3, ROWS, LANES), f32)
+    table = pltpu.VMEM((2, 2 * NX, NY, NZ * 3, ROWS, LANES), f32)
     dma = pltpu.SemaphoreType.DMA
     return pl.pallas_call(
         gather_kernel,
@@ -306,8 +341,9 @@
             pltpu.VMEM((3, 8, LANES), f32),
             pltpu.VMEM((1, 8, LANES), f32),
             pltpu.VMEM((NX, 8, LANES), f32),
-            pltpu.VMEM((3, LANES, LANES), f32),
-            pltpu.VMEM((4, LANES, LANES), f32),
+            pltpu.VMEM((4, 3, LANES, LANES), f32),
+            pltpu.VMEM((4, 4, LANES, LANES), f32),
+            pltpu.SMEM((4, 64), jnp.int32),
             pltpu.SMEM((16, 64), jnp.int32),
             pltpu.VMEM((3, 4 * LANES), f32),
             pltpu.VMEM((3, 4 * LANES), f32),
@@ -391,7 +427,9 @@
 
 
 def weight(d):
-    inv = 1.0 / (dot3(d, d) + smoothing)
+    q = dot3(d, d) + smoothing
+    inv = pl.reciprocal(q, approx=True)
+    inv = inv * (2.0 - q * inv)
     return inv * inv
 
 

time: 72.9 us -> 62.7 us (0.86)
  the two profiles are of different devices: /device:TPU:42 before, /device:TPU:5 now
where the time goes in v4:
time: 62.7 us; the launch traced here: 62.4 us
  Pallas kernels  58.1 us (93%)
  local copies, waits for them, and re-layouts  3.7 us (6%)
  between operations  0.66 us (1%)
    pallas_call x1, Pallas kernels, displace_and_list(): pl.pallas_call(gather_kernel, name='displace', out_shape=(jax.ShapeDtypeS...  42.7 us
    pallas_call x1, Pallas kernels, wall(): pl.pallas_call(wall_kernel, name='wall', out_shape=(jax.ShapeDtypeStruct(...  15.4 us
    unnamed x12, local copies, waits for them, and re-layouts  3.7 us

profile of v4, /device:TPU:5, one launch (start us, length us, event | category | flops | bytes accessed | tf_op | source)
XLA Modules:
  0.0 62.4 jit_solution(15777706223745993309)
XLA Ops:
  0.6 0.0 copy-start
  0.6 0.9 %copy-done = f32[3,8192]{1,0:T(4,128)S(1)} copy-done((f32[3,8192]{1,0:T(4,128)S(1)}, f32[3,8192]{1,0:T(4,128)}, u32[]{:S(2)}) %copy-start) | copy-done | bytes 98328
  1.5 0.0 copy-start.1
  1.5 0.7 %copy-done.1 = s32[64,16]{0,1:T(8,128)S(1)} copy-done((s32[64,16]{0,1:T(8,128)S(1)}, s32[64,16]{0,1:T(8,128)}, u32[]{:S(2)}) %copy-start.1) | copy-done | bytes 4120
  2.2 0.0 copy-start.3
  2.2 0.7 %copy-done.3 = s32[2,3,512]{2,0,1:T(2,128)S(1)} copy-done((s32[2,3,512]{2,0,1:T(2,128)S(1)}, s32[2,3,512]{2,0,1:T(2,128)}, u32[]{:S(2)}) %copy-start.3) | copy-done | bytes 12312
  2.9 0.0 copy-start.4
  2.9 0.7 %copy-done.4 = f32[3,512]{1,0:T(4,128)S(1)} copy-done((f32[3,512]{1,0:T(4,128)S(1)}, f32[3,512]{1,0:T(4,128)}, u32[]{:S(2)}) %copy-start.4) | copy-done | bytes 6168
  3.6 0.0 copy-start.5
  3.6 0.7 %copy-done.5 = f32[3,512]{1,0:T(4,128)S(1)} copy-done((f32[3,512]{1,0:T(4,128)S(1)}, f32[3,512]{1,0:T(4,128)}, u32[]{:S(2)}) %copy-start.5) | copy-done | bytes 6168
  4.3 0.0 copy-start.2
  4.3 42.7 %displace.1 = (f32[64,6,4,128]{3,2,1,0:T(4,128)S(1)}, f32[3,512]{1,0:T(4,128)S(1)}, f32[3,512]{1,0:T(4,128)S(1)}) custom-call(s32[16,64]{1,0:T(8,128)S(1)} %bitcast.4, f32[3,512]{1,0:T(4,128)S(1)} %copy-done.4, f32[3,512]{1,0:T(4,128)S(1)} %copy-done.5, s32[3,2,512]{2,1,0:T(2,128)S(1)} %bitcast.7, f32[3,8192]{1,0:T(4,128)S(1)} %copy-done), custom_call_target="tpu_custom_call" | custom-call | tf_op jit(solution)/shard_map/displace/pallas_call | solution.py:326
  47.0 0.0 copy-done.2
  47.0 15.4 %wall.1 = (f32[3,512]{1,0:T(4,128)}, f32[4,128]{1,0:T(4,128)}) custom-call(s32[16,64]{1,0:T(8,128)S(1)} %bitcast.5, f32[64,6,4,128]{3,2,1,0:T(4,128)S(1)} %get-tuple-element.7.listed_ref, f32[3,512]{1,0:T(4,128)S(1)} %get-tuple-element.8.disp_in, f32[3,512]{1,0:T(4,128)S(1)} %get-tuple-element.9.target_ref, s32[64,128]{1,0:T(8,128)S(1)} %bitcast.6), custom_call_target="tpu_custom_call" | custom-call | tf_op jit(solution)/shard_map/wall/pallas_call | solution.py:562
Async XLA Ops:
  0.6 0.9 %copy-start = (f32[3,8192]{1,0:T(4,128)S(1)}, f32[3,8192]{1,0:T(4,128)}, u32[]{:S(2)}) copy-start(f32[3,8192]{1,0:T(4,128)} %vol_hbm.1) | copy-start | bytes 294916
  1.5 0.7 %copy-start.1 = (s32[64,16]{0,1:T(8,128)S(1)}, s32[64,16]{0,1:T(8,128)}, u32[]{:S(2)}) copy-start(s32[64,16]{0,1:T(8,128)} %param.11) | copy-start | bytes 12292
  2.2 0.7 %copy-start.3 = (s32[2,3,512]{2,0,1:T(2,128)S(1)}, s32[2,3,512]{2,0,1:T(2,128)}, u32[]{:S(2)}) copy-start(s32[2,3,512]{2,0,1:T(2,128)} %param.8) | copy-start | bytes 36868
  2.9 0.7 %copy-start.4 = (f32[3,512]{1,0:T(4,128)S(1)}, f32[3,512]{1,0:T(4,128)}, u32[]{:S(2)}) copy-start(f32[3,512]{1,0:T(4,128)} %points_hbm.1) | copy-start | bytes 18436
  3.6 0.7 %copy-start.5 = (f32[3,512]{1,0:T(4,128)S(1)}, f32[3,512]{1,0:T(4,128)}, u32[]{:S(2)}) copy-start(f32[3,512]{1,0:T(4,128)} %shift_hbm.1) | copy-start | bytes 18436
  4.3 42.7 %copy-start.2 = (s32[8192]{0:T(1024)S(1)}, s32[8192]{0:T(1024)}, u32[]{:S(2)}) copy-start(s32[8192]{0:T(1024)} %param.10) | copy-start | bytes 98308

commit v5 on v4

--- a/solution.py
+++ b/solution.py
@@ -137,26 +137,50 @@
     def issue(which, part, phase):
         axis = WAYS[part][phase]
         mine = span(tables[which], part, phase, me)
-        for k in (1, 3) if phase == 2 else NEAR_FIRST[SIZES[axis]]:
+        if phase == 2:
+            for turn in range(2):
+                for k in (1, 3):
+                    piece = half_span(tables[which], part, me, (k // 2) ^ turn)
+                    start(remote(piece, piece, shifted(me, axis, k), *sems(which, part, 2, k + 4 * turn - 1)))
+            return
+        for k in NEAR_FIRST[SIZES[axis]]:
             start(remote(mine, mine, shifted(me, axis, k), *sems(which, part, phase, k)))
 
-    def collect(which, part, phase, steps=None):
+    def collect(which, part, phase):
         axis = WAYS[part][phase]
-        for k in steps or NEAR_FIRST[SIZES[axis]]:
+        for k in NEAR_FIRST[SIZES[axis]]:
             frm = shifted(me, axis, -k)
             theirs = span(tables[which], part, phase, frm)
             remote(theirs, theirs, frm, *sems(which, part, phase, k)).wait_recv()
 
+    def collect_turn(which, part, k, turn):
+        axis = WAYS[part][2]
+        frm = shifted(me, axis, -k)
+        piece = half_span(tables[which], part, frm, (k // 2) ^ turn)
+        remote(piece, piece, frm, *sems(which, part, 2, k + 4 * turn - 1)).wait_recv()
+
     def forward(which, part, k):
         axis = WAYS[part][2]
         piece = half_span(tables[which], part, shifted(me, axis, -k), k // 2)
-        start(remote(piece, piece, shifted(me, axis, k), *sems(which, part, 2, k - 1)))
+        start(remote(piece, piece, shifted(me, axis, k), *sems(which, part, 2, k)))
+
+    def pass_on(which):
+        for k in (1, 3):
+            for part in range(2):
+                collect_turn(which, part, k, 0)
+                forward(which, part, k)
+
+    def take_rest(which):
+        for k in (1, 3):
+            for part in range(2):
+                collect_turn(which, part, k, 1)
+                to_sibling(which, part, k)
 
     def collect_halves(which, part):
         axis = WAYS[part][2]
         for k in (1, 3):
             piece = half_span(tables[which], part, shifted(me, axis, 2), k // 2)
-            remote(piece, piece, shifted(me, axis, -k), *sems(which, part, 2, k - 1)).wait_recv()
+            remote(piece, piece, shifted(me, axis, -k), *sems(which, part, 2, k)).wait_recv()
 
     def to_sibling(which, part, k):
         mine = span(tables[which], part, 2, shifted(me, WAYS[part][2], -k))
@@ -245,11 +269,8 @@
         return carry
 
     lax.fori_loop(0, 4, far, 0)
-    for k in (1, 3):
-        for part in range(2):
-            collect(0, part, 2, (k,))
-            forward(0, part, k)
-            to_sibling(0, part, k)
+    pass_on(0)
+    take_rest(0)
     for part in range(2):
         issue(1, part, 2)
     for part in range(2):
@@ -292,11 +313,8 @@
             target_ref[pl.ds(c, 1), out_lanes] = vol_ref[pl.ds(c, 1), out_lanes] + disp
 
     displace(0)
-    for k in (1, 3):
-        for part in range(2):
-            collect(1, part, 2, (k,))
-            forward(1, part, k)
-            to_sibling(1, part, k)
+    pass_on(1)
+    take_rest(1)
     displace(1)
     displace(2)
     for part in range(2):
@@ -358,7 +376,7 @@
             dma((14,)),
         ],
         compiler_params=pltpu.CompilerParams(
-            collective_id=0, has_side_effects=True, vmem_limit_bytes=24 * 2**20
+            collective_id=0, has_side_effects=True, vmem_limit_bytes=60 * 2**20
         ),
     )(candidates, points, shift, facets, vol)
 
@@ -405,7 +423,7 @@
     bx, by = bc_x * inv_bc, cy * inv_bc
     ax, ay = cx * inv_ac, cy * inv_ac
     return [*e1, -dot3(e1, a), *e2, -dot3(e2, a), *n, -dot3(n, a),
-            ab_len, bx, by, bx * ab_len, by * ab_len, bc_len, ax, ay, ac_len]
+            ab_len, bx, by, bc_len, ax, ay, ac_len]
 
 
 def facet_square(p, k):
@@ -413,10 +431,11 @@
     u = px * k[0] + py * k[1] + (pz * k[2] + k[3])
     v = px * k[4] + py * k[5] + (pz * k[6] + k[7])
     h = px * k[8] + py * k[9] + (pz * k[10] + k[11])
-    ab, bx, by, bxl, byl, bc, ax, ay, ac = k[12:21]
-    r1 = u - jnp.clip(u, 0.0, ab)
-    t2 = bx * u + by * v - bxl
-    s2 = bx * v - by * u + byl
+    ab, bx, by, bc, ax, ay, ac = k[12:]
+    past = u - ab
+    r1 = jnp.maximum(jnp.maximum(past, -u), 0.0)
+    t2 = bx * past + by * v
+    s2 = bx * v - by * past
     r2 = t2 - jnp.clip(t2, 0.0, bc)
     t3 = ax * u + ay * v
     s3 = ay * u - ax * v
@@ -437,13 +456,19 @@
     return jnp.transpose(jnp.broadcast_to(row, (LANES, LANES)))
 
 
-def wall_kernel(cand_hbm, listed_ref, disp_in, target_ref, flag_ref, disp_ref, wall_ref,
-                cols, moved, index, const, best, cand_ref, in_sem):
+def wall_kernel(cand_hbm, listed_hbm, target_hbm, flag_hbm, wall_ref,
+                cols, moved, index, const, best, cand_ref, listed_ref, target_ref, flag_ref, in_sem):
     surf = lax.axis_index("surf")
-    copy = pltpu.make_async_copy(cand_hbm, cand_ref, in_sem)
-    copy.start()
-    disp_ref[...] = disp_in[...]
-    copy.wait()
+    inputs = [
+        pltpu.make_async_copy(cand_hbm, cand_ref, in_sem.at[0]),
+        pltpu.make_async_copy(listed_hbm, listed_ref, in_sem.at[1]),
+        pltpu.make_async_copy(target_hbm, target_ref, in_sem.at[2]),
+        pltpu.make_async_copy(flag_hbm, flag_ref, in_sem.at[3]),
+    ]
+    for copy in inputs:
+        copy.start()
+    for copy in inputs:
+        copy.wait()
 
     def one_block(block, carry):
         row = surf * 4 + block
@@ -491,7 +516,7 @@
 
             def one_leaf(j):
                 for quarter in range(4):
-                    k = [jnp.broadcast_to(const[i, quarter, pl.ds(j, 1), :], (8, LANES)) for i in range(21)]
+                    k = [jnp.broadcast_to(const[i, quarter, pl.ds(j, 1), :], (8, LANES)) for i in range(19)]
                     for g in range(16):
                         part = pl.ds(g * 8, 8)
                         p = [cols[c, part, :] for c in range(3)]
@@ -556,38 +581,36 @@
     lax.fori_loop(0, 4, one_block, 0)
 
 
-def wall(candidates, listed, disp, target, flags):
+def wall(candidates, listed, target, flags):
     f32 = jnp.float32
-    vmem = pl.BlockSpec(memory_space=pltpu.VMEM)
     return pl.pallas_call(
         wall_kernel,
         name="wall",
-        out_shape=(
-            jax.ShapeDtypeStruct((3, 4 * LANES), f32),
-            jax.ShapeDtypeStruct((4, LANES), f32),
-        ),
-        in_specs=[pl.BlockSpec(memory_space=pltpu.HBM), vmem, vmem, vmem, vmem],
-        out_specs=(vmem, vmem),
+        out_shape=jax.ShapeDtypeStruct((4, LANES), f32),
+        in_specs=[pl.BlockSpec(memory_space=pltpu.HBM)] * 4,
+        out_specs=pl.BlockSpec(memory_space=pltpu.VMEM),
         scratch_shapes=[
             pltpu.VMEM((3, LANES, LANES), f32),
             pltpu.VMEM((3, 2, 16, LANES), f32),
             pltpu.VMEM((3, 4, 16, LANES), jnp.int32),
-            pltpu.VMEM((21, 4, 16, LANES), f32),
+            pltpu.VMEM((19, 4, 16, LANES), f32),
             pltpu.VMEM((LANES, LANES), f32),
             pltpu.SMEM((16, 64), jnp.int32),
-            pltpu.SemaphoreType.DMA,
+            pltpu.VMEM((64, 6, ROWS, LANES), f32),
+            pltpu.VMEM((3, 4 * LANES), f32),
+            pltpu.VMEM((64, LANES), jnp.int32),
+            pltpu.SemaphoreType.DMA((4,)),
         ],
-        compiler_params=pltpu.CompilerParams(vmem_limit_bytes=24 * 2**20),
-    )(candidates, listed, disp, target, flags)
+        compiler_params=pltpu.CompilerParams(vmem_limit_bytes=60 * 2**20),
+    )(candidates, listed, target, flags)
 
 
 def body(surface_points, surface_shift, facet_nodes, volume_points, near_wall, candidates):
     candidates = candidates.T
-    listed, disp, target = displace_and_list(
+    listed, displacement, target = displace_and_list(
         candidates, surface_points, surface_shift, jnp.transpose(facet_nodes, (1, 0, 2)), volume_points
     )
-    flags = near_wall.reshape(-1, LANES)
-    displacement, distance = wall(candidates, listed, disp, target, flags)
+    distance = wall(candidates, listed, target, near_wall.reshape(-1, LANES))
     return displacement, distance.reshape(-1)
 
 

time: 62.7 us -> 66 us (1.053)
  the two profiles are of different devices: /device:TPU:5 before, /device:TPU:1 now
where the time goes in v5:
time: 66 us; the launch traced here: 65.9 us
  Pallas kernels  64.6 us (98%)
  between operations  0.66 us (1%)
    pallas_call x1, Pallas kernels, displace_and_list(): pl.pallas_call(gather_kernel, name='displace', out_shape=(jax.ShapeDtypeS...  46.3 us
    pallas_call x1, Pallas kernels, wall(): pl.pallas_call(wall_kernel, name='wall', out_shape=jax.ShapeDtypeStruct((...  18.3 us

profile of v5, /device:TPU:1, one launch (start us, length us, event | category | flops | bytes accessed | tf_op | source)
XLA Modules:
  0.0 65.9 jit_solution(15595218900076445441)
XLA Ops:
  0.6 46.3 %displace.1 = (f32[64,6,4,128]{3,2,1,0:T(4,128)}, f32[3,512]{1,0:T(4,128)}, f32[3,512]{1,0:T(4,128)}) custom-call(s32[16,64]{1,0:T(8,128)} %bitcast.4, f32[3,512]{1,0:T(4,128)} %points_hbm.1, f32[3,512]{1,0:T(4,128)} %shift_hbm.1, s32[3,2,512]{2,1,0:T(2,128)} %bitcast.7, f32[3,8192]{1,0:T(4,128)} %vol_hbm.1), custom_call_target="tpu_custom_call" | custom-call | tf_op jit(solution)/shard_map/displace/pallas_call | solution.py:344
  46.9 0.0 copy-start
  46.9 18.3 %wall.1 = f32[4,128]{1,0:T(4,128)} custom-call(s32[16,64]{1,0:T(8,128)} %bitcast.5, f32[64,6,4,128]{3,2,1,0:T(4,128)} %get-tuple-element.6.listed_hbm, f32[3,512]{1,0:T(4,128)} %get-tuple-element.7.target_hbm, s32[64,128]{1,0:T(8,128)} %bitcast.6), custom_call_target="tpu_custom_call" | custom-call | tf_op jit(solution)/shard_map/wall/pallas_call | solution.py:586
  65.3 0.0 copy-done
  65.3 0.6 copy.9
Async XLA Ops:
  46.9 18.3 %copy-start = (f32[3,512]{1,0:T(4,128)S(1)}, f32[3,512]{1,0:T(4,128)}, u32[]{:S(2)}) copy-start(f32[3,512]{1,0:T(4,128)} %get-tuple-element.10) | copy-start | bytes 18436

commit v6 on v5

--- a/solution.py
+++ b/solution.py
@@ -407,6 +407,14 @@
 
 
 def facet_constants(a, b, c):
+    sides = [dot3(d, d) for d in (minus3(b, a), minus3(c, b), minus3(a, c))]
+    bc_long = (sides[1] > sides[0]) & (sides[1] >= sides[2])
+    ca_long = (sides[2] > sides[0]) & (sides[2] > sides[1])
+
+    def pick(p, q, r):
+        return [jnp.where(bc_long, q[i], jnp.where(ca_long, r[i], p[i])) for i in range(3)]
+
+    a, b, c = pick(a, b, c), pick(b, c, a), pick(c, a, b)
     ab, ac = minus3(b, a), minus3(c, a)
     normal = cross3(ab, ac)
     ab_len = jnp.sqrt(dot3(ab, ab))
@@ -415,15 +423,14 @@
     e1 = [q * inv_ab for q in ab]
     n = [q * inv_n for q in normal]
     e2 = cross3(n, e1)
-    cx, cy = dot3(ac, e1), dot3(ac, e2)
-    bc_x = cx - ab_len
-    bc_len = jnp.sqrt(bc_x * bc_x + cy * cy)
-    ac_len = jnp.sqrt(cx * cx + cy * cy)
-    inv_bc, inv_ac = 1.0 / bc_len, 1.0 / ac_len
-    bx, by = bc_x * inv_bc, cy * inv_bc
-    ax, ay = cx * inv_ac, cy * inv_ac
-    return [*e1, -dot3(e1, a), *e2, -dot3(e2, a), *n, -dot3(n, a),
-            ab_len, bx, by, bc_len, ax, ay, ac_len]
+    top = dot3(ac, e2)
+    left = dot3(ac, e1)
+    out = [*e1, -dot3(e1, a) - left, *e2, -dot3(e2, a), *n, -dot3(n, a)]
+    for foot in (left, ab_len - left):
+        leg = jnp.sqrt(foot * foot + top * top)
+        inv_leg = 1.0 / leg
+        out += [foot, top * inv_leg, foot * inv_leg, leg]
+    return out
 
 
 def facet_square(p, k):
@@ -431,18 +438,16 @@
     u = px * k[0] + py * k[1] + (pz * k[2] + k[3])
     v = px * k[4] + py * k[5] + (pz * k[6] + k[7])
     h = px * k[8] + py * k[9] + (pz * k[10] + k[11])
-    ab, bx, by, bc, ax, ay, ac = k[12:]
-    past = u - ab
-    r1 = jnp.maximum(jnp.maximum(past, -u), 0.0)
-    t2 = bx * past + by * v
-    s2 = bx * v - by * past
-    r2 = t2 - jnp.clip(t2, 0.0, bc)
-    t3 = ax * u + ay * v
-    s3 = ay * u - ax * v
-    r3 = t3 - jnp.clip(t3, 0.0, ac)
-    edge = jnp.minimum(jnp.minimum(r1 * r1 + v * v, r2 * r2 + s2 * s2), r3 * r3 + s3 * s3)
-    inside = jnp.minimum(jnp.minimum(v, s2), s3) >= 0.0
-    return h * h + jnp.where(inside, 0.0, edge)
+    on_left = u < 0.0
+    foot, rise, run, leg = (jnp.where(on_left, k[12 + i], k[16 + i]) for i in range(4))
+    past = jnp.abs(u) - foot
+    s = past * rise + v * run
+    t = v * rise - past * run
+    below = v < 0.0
+    across = jnp.where(below, past, s)
+    across = jnp.maximum(across, 0.0)
+    along = jnp.where(below, v, t - jnp.clip(t, 0.0, leg))
+    return h * h + (across * across + along * along)
 
 
 def weight(d):
@@ -516,7 +521,7 @@
 
             def one_leaf(j):
                 for quarter in range(4):
-                    k = [jnp.broadcast_to(const[i, quarter, pl.ds(j, 1), :], (8, LANES)) for i in range(19)]
+                    k = [jnp.broadcast_to(const[i, quarter, pl.ds(j, 1), :], (8, LANES)) for i in range(20)]
                     for g in range(16):
                         part = pl.ds(g * 8, 8)
                         p = [cols[c, part, :] for c in range(3)]
@@ -593,7 +598,7 @@
             pltpu.VMEM((3, LANES, LANES), f32),
             pltpu.VMEM((3, 2, 16, LANES), f32),
             pltpu.VMEM((3, 4, 16, LANES), jnp.int32),
-            pltpu.VMEM((19, 4, 16, LANES), f32),
+            pltpu.VMEM((20, 4, 16, LANES), f32),
             pltpu.VMEM((LANES, LANES), f32),
             pltpu.SMEM((16, 64), jnp.int32),
             pltpu.VMEM((64, 6, ROWS, LANES), f32),

time: 66 us -> 60.2 us (0.912)
  the two profiles are of different devices: /device:TPU:1 before, /device:TPU:37 now
where the time goes in v6:
time: 60.2 us; the launch traced here: 60.1 us
  Pallas kernels  58.8 us (98%)
  between operations  0.66 us (1%)
  local copies, waits for them, and re-layouts  0.61 us (1%)
    pallas_call x1, Pallas kernels, displace_and_list(): pl.pallas_call(gather_kernel, name='displace', out_shape=(jax.ShapeDtypeS...  44.1 us
    pallas_call x1, Pallas kernels, wall(): pl.pallas_call(wall_kernel, name='wall', out_shape=jax.ShapeDtypeStruct((...  14.7 us

profile of v6, /device:TPU:37, one launch (start us, length us, event | category | flops | bytes accessed | tf_op | source)
XLA Modules:
  0.0 60.1 jit_solution(6513826482371377064)
XLA Ops:
  0.6 44.1 %displace.1 = (f32[64,6,4,128]{3,2,1,0:T(4,128)}, f32[3,512]{1,0:T(4,128)}, f32[3,512]{1,0:T(4,128)}) custom-call(s32[16,64]{1,0:T(8,128)} %bitcast.4, f32[3,512]{1,0:T(4,128)} %points_hbm.1, f32[3,512]{1,0:T(4,128)} %shift_hbm.1, s32[3,2,512]{2,1,0:T(2,128)} %bitcast.7, f32[3,8192]{1,0:T(4,128)} %vol_hbm.1), custom_call_target="tpu_custom_call" | custom-call | tf_op jit(solution)/shard_map/displace/pallas_call | solution.py:344
  44.8 0.0 copy-start
  44.8 14.7 %wall.1 = f32[4,128]{1,0:T(4,128)} custom-call(s32[16,64]{1,0:T(8,128)} %bitcast.5, f32[64,6,4,128]{3,2,1,0:T(4,128)} %get-tuple-element.6.listed_hbm, f32[3,512]{1,0:T(4,128)} %get-tuple-element.7.target_hbm, s32[64,128]{1,0:T(8,128)} %bitcast.6), custom_call_target="tpu_custom_call" | custom-call | tf_op jit(solution)/shard_map/wall/pallas_call | solution.py:591
  59.5 0.0 copy-done
  59.5 0.6 %copy.9 = f32[3,512]{1,0:T(4,128)} copy(f32[3,512]{1,0:T(4,128)S(1)} %copy-done) | data formatting | bytes 12288
Async XLA Ops:
  44.8 14.7 %copy-start = (f32[3,512]{1,0:T(4,128)S(1)}, f32[3,512]{1,0:T(4,128)}, u32[]{:S(2)}) copy-start(f32[3,512]{1,0:T(4,128)} %get-tuple-element.10) | copy-start | bytes 18436

commit v7 on v6

--- a/solution.py
+++ b/solution.py
@@ -207,31 +207,23 @@
     mom = mom_copies(mom_z, [shifted(me, "z", k) for k in range(1, NZ)], 0)
     for copy in mom:
         copy.start()
-    issue(1, 0, 0)
     collect(0, 0, 0)
     issue(0, 0, 1)
     issue(0, 1, 1)
+    issue(1, 0, 0)
     mom_sum(mom, mom_z)
     mom = mom_copies(mom_y, [shifted(me, "y", k) for k in range(1, NY)], 7)
     for copy in mom:
         copy.start()
-    collect(1, 0, 0)
-    issue(1, 0, 1)
-    issue(1, 1, 1)
     for part in range(2):
         collect(0, part, 1)
         issue(0, part, 2)
-    for part in range(2):
-        to_sibling(0, part, 0)
     mom_sum(mom, mom_y)
     mom = mom_copies(mom_c, [sibling], 10)
     mom[0].start()
     for part in range(2):
-        collect(1, part, 1)
-    mom_sum(mom, mom_c)
-    moments[pl.ds(me["x"], 1)] = mom_own[...][None]
-    for k in range(1, NX):
-        start(remote(mom_own, moments.at[me["x"]], shifted(me, "x", k), mom_send.at[10 + k], mom_recv.at[10 + k]))
+        to_sibling(0, part, 0)
+
     def locate(n, carry):
         at = leaf_index(jnp.maximum(cand_ref[n % 16, surf * 4 + n // 16], 0))
         for i in range(4):
@@ -239,9 +231,17 @@
         return carry
 
     lax.fori_loop(0, 64, locate, 0)
+    mom_sum(mom, mom_c)
+    moments[pl.ds(me["x"], 1)] = mom_own[...][None]
+    for k in range(1, NX):
+        start(remote(mom_own, moments.at[me["x"]], shifted(me, "x", k), mom_send.at[10 + k], mom_recv.at[10 + k]))
+    collect(1, 0, 0)
+    issue(1, 0, 1)
+    issue(1, 1, 1)
     for block in range(4):
         for c in range(3):
             cols[block, c] = as_columns(vol_ref[pl.ds(c, 1), pl.ds(block * LANES, LANES)])
+    pass_on(0)
     for k in range(1, NX):
         frm = shifted(me, "x", -k)
         remote(mom_own, moments.at[frm["x"]], frm, mom_send.at[10 + k], mom_recv.at[10 + k]).wait_recv()
@@ -269,9 +269,9 @@
         return carry
 
     lax.fori_loop(0, 4, far, 0)
-    pass_on(0)
     take_rest(0)
     for part in range(2):
+        collect(1, part, 1)
         issue(1, part, 2)
     for part in range(2):
         collect_halves(0, part)
@@ -461,7 +461,7 @@
     return jnp.transpose(jnp.broadcast_to(row, (LANES, LANES)))
 
 
-def wall_kernel(cand_hbm, listed_hbm, target_hbm, flag_hbm, wall_ref,
+def wall_kernel(cand_hbm, listed_hbm, target_hbm, flag_hbm, disp_hbm, disp_out, wall_ref,
                 cols, moved, index, const, best, cand_ref, listed_ref, target_ref, flag_ref, in_sem):
     surf = lax.axis_index("surf")
     inputs = [
@@ -470,8 +470,10 @@
         pltpu.make_async_copy(target_hbm, target_ref, in_sem.at[2]),
         pltpu.make_async_copy(flag_hbm, flag_ref, in_sem.at[3]),
     ]
+    hand_over = pltpu.make_async_copy(disp_hbm, disp_out, in_sem.at[4])
     for copy in inputs:
         copy.start()
+    hand_over.start()
     for copy in inputs:
         copy.wait()
 
@@ -584,16 +586,21 @@
         return carry
 
     lax.fori_loop(0, 4, one_block, 0)
-
-
-def wall(candidates, listed, target, flags):
+    hand_over.wait()
+
+
+def wall(candidates, listed, target, flags, displacement):
     f32 = jnp.float32
+    hbm = pl.BlockSpec(memory_space=pltpu.HBM)
     return pl.pallas_call(
         wall_kernel,
         name="wall",
-        out_shape=jax.ShapeDtypeStruct((4, LANES), f32),
-        in_specs=[pl.BlockSpec(memory_space=pltpu.HBM)] * 4,
-        out_specs=pl.BlockSpec(memory_space=pltpu.VMEM),
+        out_shape=(
+            jax.ShapeDtypeStruct((3, 4 * LANES), f32),
+            jax.ShapeDtypeStruct((4, LANES), f32),
+        ),
+        in_specs=[hbm] * 5,
+        out_specs=(hbm, pl.BlockSpec(memory_space=pltpu.VMEM)),
         scratch_shapes=[
             pltpu.VMEM((3, LANES, LANES), f32),
             pltpu.VMEM((3, 2, 16, LANES), f32),
@@ -604,10 +611,10 @@
             pltpu.VMEM((64, 6, ROWS, LANES), f32),
             pltpu.VMEM((3, 4 * LANES), f32),
             pltpu.VMEM((64, LANES), jnp.int32),
-            pltpu.SemaphoreType.DMA((4,)),
+            pltpu.SemaphoreType.DMA((5,)),
         ],
         compiler_params=pltpu.CompilerParams(vmem_limit_bytes=60 * 2**20),
-    )(candidates, listed, target, flags)
+    )(candidates, listed, target, flags, displacement)
 
 
 def body(surface_points, surface_shift, facet_nodes, volume_points, near_wall, candidates):
@@ -615,7 +622,7 @@
     listed, displacement, target = displace_and_list(
         candidates, surface_points, surface_shift, jnp.transpose(facet_nodes, (1, 0, 2)), volume_points
     )
-    distance = wall(candidates, listed, target, near_wall.reshape(-1, LANES))
+    displacement, distance = wall(candidates, listed, target, near_wall.reshape(-1, LANES), displacement)
     return displacement, distance.reshape(-1)
 
 

time: 60.2 us -> 59.6 us (0.990)
  the two profiles are of different devices: /device:TPU:37 before, /device:TPU:0 now
where the time goes in v7:
time: 59.6 us; the launch traced here: 59.4 us
  Pallas kernels  58.7 us (98%)
  between operations  0.64 us (1%)
    pallas_call x1, Pallas kernels, displace_and_list(): pl.pallas_call(gather_kernel, name='displace', out_shape=(jax.ShapeDtypeS...  41.5 us
    pallas_call x1, Pallas kernels, wall(): pl.pallas_call(wall_kernel, name='wall', out_shape=(jax.ShapeDtypeStruct(...  17.2 us

profile of v7, /device:TPU:0, one launch (start us, length us, event | category | flops | bytes accessed | tf_op | source)
XLA Modules:
  0.0 59.4 jit_solution(1319322417227282032)
XLA Ops:
  0.6 41.5 %displace.1 = (f32[64,6,4,128]{3,2,1,0:T(4,128)}, f32[3,512]{1,0:T(4,128)}, f32[3,512]{1,0:T(4,128)}) custom-call(s32[16,64]{1,0:T(8,128)} %bitcast.4, f32[3,512]{1,0:T(4,128)} %points_hbm.1, f32[3,512]{1,0:T(4,128)} %shift_hbm.1, s32[3,2,512]{2,1,0:T(2,128)} %bitcast.7, f32[3,8192]{1,0:T(4,128)} %vol_hbm.1), custom_call_target="tpu_custom_call" | custom-call | tf_op jit(solution)/shard_map/displace/pallas_call | solution.py:344
  42.1 17.2 %wall.1 = (f32[3,512]{1,0:T(4,128)}, f32[4,128]{1,0:T(4,128)}) custom-call(s32[16,64]{1,0:T(8,128)} %bitcast.5, f32[64,6,4,128]{3,2,1,0:T(4,128)} %get-tuple-element.7.listed_hbm, f32[3,512]{1,0:T(4,128)} %get-tuple-element.8.target_hbm, s32[64,128]{1,0:T(8,128)} %bitcast.6, f32[3,512]{1,0:T(4,128)} %get-tuple-element.9.disp_hbm), custom_call_target="tpu_custom_call" | custom-call | tf_op jit(solution)/shard_map/wall/pallas_call | solution.py:595
